TPU v7x, 32 devices: a whole 2x2x4 slice. The times are simulated.
32 devices in a mesh: node: 2 (over core), trow: 4 (over y, x), tcol: 4 (over z).
Axes of the slice: x: 2, y: 2, z: 4, core: 2. Of those that a mesh axis runs over, the one named last changes fastest.
Arguments:
- near_blocks: bfloat16 [128, 8, 256, 256], P(('node', 'trow'), 'tcol'), may hold values from -27 to 75, as said below
- leaf_bases: bfloat16 [128, 256, 256], P(('node', 'trow')), may hold values from -1 to 1, as said below
- upper_bases: bfloat16 [64, 256, 256], P(('node', 'trow', 'tcol')), may hold values from -1 to 1, as said below
- neighbours: int32 [128, 8], P(('node', 'trow'), 'tcol'), may hold values from 0 to 127, as said below
Outputs:
- skeleton: float32 [128, 8, 128, 128], P(('node', 'trow'), 'tcol')
- upper_skeleton: float32 [64, 5, 128, 128], P(('node', 'trow', 'tcol'))
Inputs may be any that keep to these rules, and one draw needn't show every extreme that they name: `neighbours`: slot 0 of row i is i, slot 1 is its sibling i XOR 1, and slots 2 to 7 are six distinct leaves among 2 (i // 2) - 4, -3, -2, -1, +2, +3, +4, +5, taken modulo 128. near_blocks[i, 0] is symmetric and positive definite. `leaf_bases`: each leaf basis is an orthogonal matrix rounded to bfloat16. `upper_bases`: each node basis is an orthogonal matrix rounded to bfloat16.
All inputs are finite; a program needn't handle non-finite values.
Results may differ from a plain program's by a relative error of at most 0.0038.
Values may be sent and summed in bfloat16 or wider, within the bound.
No kernel may reach another device: no remote copies, remote signals or barrier semaphores. Data moves between devices by JAX's collectives and lax.ppermute only.
A program may use at most 64 MiB of HBM per device.

v0:
```python
import jax
import jax.numpy as jnp
from jax import lax
from jax.sharding import PartitionSpec as P

BLK = 256
RANK = 128


def with_halo(array, sides, width):
    for axis, dim in sides:
        count, length = (lax.axis_size(axis), array.shape[dim])
        up = [(i, (i + 1) % count) for i in range(count)]
        down = [(j, i) for i, j in up]
        last = lax.slice_in_dim(array, length - width, length, axis=dim)
        initial = lax.slice_in_dim(array, 0, width, axis=dim)
        before = lax.ppermute(last, axis, up)
        after = lax.ppermute(initial, axis, down)
        array = jnp.concatenate([before, array, after], axis=dim)
    return array


def spread(block, axis, source):
    block = jnp.where(lax.axis_index(axis) == source, block, jnp.zeros_like(block))
    return lax.psum(block, axis)


def eliminate(rotated, spare_size):
    corner = rotated[..., :spare_size, :spare_size]
    factor = jnp.linalg.cholesky(0.5 * (corner + jnp.swapaxes(corner, -1, -2)))
    coupled = lax.linalg.triangular_solve(
        factor, rotated[..., :spare_size, spare_size:], left_side=True, lower=True
    )
    return (factor, coupled)


def reduce_rows(rotated, factor, coupled, spare_size):
    widened = jnp.broadcast_to(factor[:, None], rotated.shape[:2] + factor.shape[1:])
    solved = lax.linalg.triangular_solve(
        widened, rotated[..., :spare_size, spare_size:], left_side=True, lower=True
    )
    return rotated[..., spare_size:, spare_size:] - jnp.einsum(
        "lxr,lkxs->lkrs", coupled, solved, precision=lax.Precision.HIGHEST
    )


def arrange(blocks, parent_count, rank_size):
    shaped = blocks.reshape(parent_count, 2, 5, 2, rank_size, rank_size)
    return shaped.transpose(0, 2, 1, 4, 3, 5).reshape(parent_count, 5, 2 * rank_size, 2 * rank_size)


def per_device(near_blocks, leaf_bases, upper_bases, neighbours):
    leaf_count = near_blocks.shape[0]
    spare_size = BLK - RANK
    leaf_total = leaf_count * lax.axis_size(("node", "trow"))
    parents_all = leaf_total // 2
    first_leaf = lax.axis_index(("node", "trow")) * leaf_count
    widened = with_halo(leaf_bases, ((("node", "trow"), 0),), 5)
    position = (neighbours - first_leaf + leaf_total // 2) % leaf_total - leaf_total // 2 + 5
    partner = widened[position]
    turned = jnp.einsum(
        "lkab,lkbc->lkac", near_blocks, partner, preferred_element_type=jnp.float32
    ).astype(jnp.bfloat16)
    rotated = jnp.einsum("lba,lkbc->lkac", leaf_bases, turned, preferred_element_type=jnp.float32)
    factor, coupled = eliminate(rotated[:, 0], spare_size)
    shared = spread(jnp.concatenate([factor, coupled], axis=2), "tcol", 0)
    skeleton = reduce_rows(
        rotated, shared[:, :, :spare_size], shared[:, :, spare_size:], spare_size
    )
    packed = skeleton.astype(jnp.bfloat16)
    leaf_ids = first_leaf + jnp.arange(leaf_count, dtype=jnp.int32)
    target = 2 * ((neighbours // 2 - leaf_ids[:, None] // 2 + 2) % parents_all) + neighbours % 2
    labels = jnp.arange(10, dtype=jnp.int32)
    arrived, arrived_target = (
        lax.all_to_all(packed, "tcol", split_axis=0, concat_axis=1, tiled=True),
        lax.all_to_all(
            target.astype(jnp.bfloat16), "tcol", split_axis=0, concat_axis=1, tiled=True
        ),
    )
    selector = (arrived_target[:, :, None] == labels.astype(jnp.bfloat16)).astype(jnp.bfloat16)
    blocks = jnp.einsum("lkc,lkxy->lcxy", selector, arrived, preferred_element_type=jnp.float32)
    merged = arrange(blocks, arrived.shape[0] // 2, RANK).astype(jnp.bfloat16)
    parent_count = upper_bases.shape[0]
    extended = with_halo(upper_bases, ((("node", "trow", "tcol"), 0),), 2)
    partners = jnp.stack([extended[offset : offset + parent_count] for offset in range(5)], axis=1)
    upper_mixed = jnp.einsum(
        "pdab,pdbc->pdac", merged, partners, preferred_element_type=jnp.float32
    ).astype(jnp.bfloat16)
    lifted = jnp.einsum(
        "pba,pdbc->pdac", upper_bases, upper_mixed, preferred_element_type=jnp.float32
    )
    upper_factor, upper_coupled = eliminate(lifted[:, 2], RANK)
    upper_skeleton = reduce_rows(lifted, upper_factor, upper_coupled, RANK)
    return (skeleton, upper_skeleton)


def solution(mesh):
    return jax.shard_map(
        per_device,
        mesh=mesh,
        in_specs=(
            P(("node", "trow"), "tcol", None, None),
            P(("node", "trow"), None, None),
            P(("node", "trow", "tcol"), None, None),
            P(("node", "trow"), "tcol"),
        ),
        out_specs=(
            P(("node", "trow"), "tcol", None, None),
            P(("node", "trow", "tcol"), None, None, None),
        ),
        check_vma=False,
    )
```

profile of v0, /device:TPU:0, one launch (start us, length us, event | category | flops | bytes accessed | tf_op | source)
XLA Modules:
  0.0 1024.9 jit_solution(10384354203430815400)
XLA Ops:
  7.2 1.4 fusion.37
  8.6 3.0 collective-permute-start
  12.4 14.4 %collective-permute-done = bf16[5,256,256]{2,1,0:T(8,128)(2,1)S(1)} collective-permute-done((bf16[5,256,256]{2,1,0:T(8,128)(2,1)S(1)}, bf16[5,256,256]{2,1,0:T(8,128)(2,1)S(1)}, u32[]{:S(2)}, u32[]{:S(2)}) %collective-permute-start) | collective-permute-done | bytes 655392 | tf_op jit(solution)/shard_map/ppermute | solution.py:17
  27.6 14.1 %collective-permute-done.1 = bf16[5,256,256]{2,1,0:T(8,128)(2,1)} collective-permute-done((bf16[5,256,256]{2,1,0:T(8,128)(2,1)S(1)}, bf16[5,256,256]{2,1,0:T(8,128)(2,1)}, u32[]{:S(2)}, u32[]{:S(2)}) %collective-permute-start.1) | collective-permute-done | bytes 655392 | tf_op jit(solution)/shard_map/ppermute | solution.py:18
  41.7 2.1 pad_maximum_fusion
  43.8 2.8 gather_fusion
  46.6 4.9 convert_bitcast_fusion
  53.2 2.7 copy-done
  56.0 2.0 copy-done.2
  58.4 1.4 fusion.15
  60.2 187.5 %custom-call.20 = f32[16,128,128]{2,1,0:T(8,128)S(1)} custom-call(f32[16,128,128]{2,1,0:T(8,128)S(1)} %fusion.14), custom_call_target="Cholesky" | custom-call | tf_op jit(solution)/shard_map/jit(cholesky)/cholesky | solution.py:30
  248.2 157.3 %custom-call.21 = f32[16,1,128,128]{2,3,1,0:T(8,128)S(1)} custom-call(f32[16,1,128,128]{3,2,1,0:T(8,128)S(1)} %get-tuple-element.12), custom_call_target="InvertDiagBlocksLowerTriangular" | custom-call | tf_op jit(solution)/shard_map/triangular_solve | solution.py:31
  405.6 3.1 fusion.11
  408.7 1.5 maximum_select_fusion
  410.9 4.9 all-to-all-start
  415.8 81.4 %all-reduce.2.cloned.1.call-done = f32[16,128,256]{2,1,0:T(8,128)} async-done(((f32[16,128,256]{2,1,0:T(8,128)}), f32[16,128,256]{2,1,0:T(8,128)}) %all-reduce.2.cloned.1.call-update) | async-done | bytes 2097168 | tf_op jit(solution)/shard_map/psum | solution.py:25
  498.4 1.6 broadcast_select_fusion
  500.0 315.1 %custom-call.22 = f32[16,2,1,128,128]{3,4,2,1,0:T(8,128)S(1)} custom-call(f32[16,2,1,128,128]{4,3,2,1,0:T(8,128)} %broadcast_select_fusion), custom_call_target="InvertDiagBlocksLowerTriangular" | custom-call | tf_op jit(solution)/shard_map/triangular_solve | solution.py:39
  815.1 3.8 fusion.5
  819.0 3.7 fusion.38
  823.8 4.3 all-to-all-start.1
  828.1 2.0 collective-permute-start.2
  830.0 3.4 collective-permute-start.3
  833.6 22.2 %collective-permute-done.2 = bf16[2,256,256]{2,1,0:T(8,128)(2,1)S(1)} collective-permute-done((bf16[2,256,256]{2,1,0:T(8,128)(2,1)S(1)}, bf16[2,256,256]{2,1,0:T(8,128)(2,1)S(1)}, u32[]{:S(2)}, u32[]{:S(2)}) %collective-permute-start.2) | collective-permute-done | bytes 262176 | tf_op jit(solution)/shard_map/ppermute | solution.py:17
  859.4 1.8 copy.96
  861.2 2.5 copy.82
  864.9 1.4 copy.84
  867.1 1.8 convolution_convert_fusion.1
  870.6 24.3 %custom-call.23 = f32[2,128,128]{2,1,0:T(8,128)S(1)} custom-call(f32[2,128,128]{2,1,0:T(8,128)} %fusion.26), custom_call_target="Cholesky" | custom-call | tf_op jit(solution)/shard_map/jit(cholesky)/cholesky | solution.py:30
  895.1 19.7 %custom-call.25 = f32[2,1,128,128]{2,3,1,0:T(8,128)S(1)} custom-call(f32[2,1,128,128]{3,2,1,0:T(8,128)S(1)} %get-tuple-element.10), custom_call_target="InvertDiagBlocksLowerTriangular" | custom-call | tf_op jit(solution)/shard_map/triangular_solve | solution.py:31
  915.2 99.2 %custom-call.24 = f32[2,5,1,128,128]{3,4,2,1,0:T(8,128)} custom-call(f32[2,5,1,128,128]{4,3,2,1,0:T(8,128)S(1)} %broadcast_select_fusion.1), custom_call_target="InvertDiagBlocksLowerTriangular" | custom-call | tf_op jit(solution)/shard_map/triangular_solve | solution.py:39
  1014.4 1.8 fusion.16
  (63 shorter events, 17.4 us)
Async XLA Ops:
  7.2 4.9 copy-start.6
  7.2 490.0 %all-reduce.2.cloned.1.call-start = ((), (), s32[]{:S(2)}) async-start(), calls=%async_computation.2 | async-start | bytes 4194304 | tf_op jit(solution)/shard_map/psum | solution.py:25
  8.6 18.1 %collective-permute-start = (bf16[5,256,256]{2,1,0:T(8,128)(2,1)S(1)}, bf16[5,256,256]{2,1,0:T(8,128)(2,1)S(1)}, u32[]{:S(2)}, u32[]{:S(2)}) collective-permute-start(bf16[5,256,256]{2,1,0:T(8,128)(2,1)S(1)} %get-tuple-element.14), channel_id=1, source_target_pairs={{0,4},{4,8},{8,12},{12,16},{16,20},{20,24},{24,28},{28,0},{1,5},{5... | collective-permute-start | bytes 1966088 | tf_op jit(solution)/shard_map/ppermute | solution.py:17
  11.6 30.1 %collective-permute-start.1 = (bf16[5,256,256]{2,1,0:T(8,128)(2,1)S(1)}, bf16[5,256,256]{2,1,0:T(8,128)(2,1)}, u32[]{:S(2)}, u32[]{:S(2)}) collective-permute-start(bf16[5,256,256]{2,1,0:T(8,128)(2,1)S(1)} %get-tuple-element.15), channel_id=1, source_target_pairs={{4,0},{8,4},{12,8},{16,12},{20,16},{24,20},{28,24},{0,28},{5,1},{9... | collective-permute-start | bytes 1966088 | tf_op jit(solution)/shard_map/ppermute | solution.py:18
  26.7 0.8 copy-start.5
  46.6 4.9 copy-start.1
  52.8 3.2 copy-start
  56.0 2.0 copy-start.2
  410.9 412.9 %all-to-all-start = ((bf16[4,4,2]{1,2,0:T(2,128)(2,1)}), bf16[4,4,2]{1,2,0:T(2,128)(2,1)S(1)}, u32[]{:S(2)}, u32[]{:S(2)}) async-start(bf16[4,4,2]{1,2,0:T(2,128)(2,1)} %copy.79), calls=%async_computation | async-start | bytes 4096 | tf_op jit(solution)/shard_map/all_to_all | solution.py:76
  497.2 1.2 slice-start
  815.1 3.8 copy-start.4
  822.7 5.3 copy-start.3
  823.8 37.5 %all-to-all-start.1 = ((bf16[16,2,128,128]{2,3,1,0:T(8,128)(2,1)}), bf16[16,2,128,128]{2,3,1,0:T(8,128)(2,1)}, u32[]{:S(2)}, u32[]{:S(2)}) async-start(bf16[16,2,128,128]{2,3,1,0:T(8,128)(2,1)} %copy.81), calls=%async_computation.1 | async-start | bytes 2097152 | tf_op jit(solution)/shard_map/all_to_all | solution.py:75
  828.1 27.7 %collective-permute-start.2 = (bf16[2,256,256]{2,1,0:T(8,128)(2,1)S(1)}, bf16[2,256,256]{2,1,0:T(8,128)(2,1)S(1)}, u32[]{:S(2)}, u32[]{:S(2)}) collective-permute-start(bf16[2,256,256]{2,1,0:T(8,128)(2,1)S(1)} %copy-done.3), channel_id=1, source_target_pairs={{0,1},{1,2},{2,3},{3,4},{4,5},{5,6},{6,7},{7,8},{8,9},{9,10},{10,1... | collective-permute-start | bytes 786440 | tf_op jit(solution)/shard_map/ppermute | solution.py:17
  830.0 27.9 %collective-permute-start.3 = (bf16[2,256,256]{2,1,0:T(8,128)(2,1)S(1)}, bf16[2,256,256]{2,1,0:T(8,128)(2,1)S(1)}, u32[]{:S(2)}, u32[]{:S(2)}) collective-permute-start(bf16[2,256,256]{2,1,0:T(8,128)(2,1)S(1)} %copy-done.3), channel_id=1, source_target_pairs={{1,0},{2,1},{3,2},{4,3},{5,4},{6,5},{7,6},{8,7},{9,8},{10,9},{11,1... | collective-permute-start | bytes 786440 | tf_op jit(solution)/shard_map/ppermute | solution.py:18
Sparse Core Ops, SparseCore 0:
  410.3 86.7 all-reduce.1
where the time goes:
time: 1030 us; the launch traced here: 1020 us
  other arithmetic  813 us (79%)
  waiting for transfers between devices  132 us (13%)
  local copies, waits for them, and re-layouts  24.5 us (2%)
  matrix products  23 us (2%)
  starting transfers between devices  18 us (2%)
  between operations  14.4 us (1%)
    another operation x5, other arithmetic, reduce_rows(): lax.linalg.triangular_solve(widened, rotated[..., :spare_size, spare_size...  416 us
    another operation x7, other arithmetic, eliminate(): factor = jnp.linalg.cholesky(0.5 * (corner + jnp.swapaxes(corner, -1, -2)))  212 us
    another operation x4, other arithmetic, eliminate(): lax.linalg.triangular_solve(factor, rotated[..., :spare_size, spare_size:...  177 us
    psum x1, waiting for transfers between devices, spread(): return lax.psum(block, axis)  81.4 us
    ppermute x2, waiting for transfers between devices, with_halo(): before = lax.ppermute(last, axis, up)  36.6 us
  transfers between devices with their start and end apart: 7, of which 4 were waited for; matrix products, arithmetic and copies ran while one was open for 32% of the time, Pallas kernels for 0%

commit v1 on v0

v1 whole, which is shorter than its diff:
```python
import functools

import jax
import jax.numpy as jnp
from jax import lax
from jax.experimental import pallas as pl
from jax.experimental.pallas import tpu as pltpu
from jax.sharding import PartitionSpec as P

BLK = 256
RANK = 128
SPARE = BLK - RANK
REACH = 4
PANEL = 32
F32 = jnp.float32
BF16 = jnp.bfloat16
VMEM = pltpu.VMEM
SMEM = pltpu.SMEM
PARAMS = pltpu.CompilerParams(vmem_limit_bytes=40 << 20)


def ring(array, axes, step):
    count = lax.axis_size(axes)
    return lax.ppermute(array, axes, [(i, (i + step) % count) for i in range(count)])


def split(x):
    high = x.astype(BF16)
    return high, (x - high.astype(F32)).astype(BF16)


def dot(a, b):
    return jnp.dot(a, b, preferred_element_type=F32)


def dot_t(a, b):
    return lax.dot_general(a, b, (((0,), (0,)), ((), ())), preferred_element_type=F32)


def dot3(a, b):
    a_high, a_low = split(a)
    b_high, b_low = split(b)
    return dot(
        jnp.concatenate([a_high, a_high, a_low], axis=1),
        jnp.concatenate([b_high, b_low, b_high], axis=0),
    )


def invert_small(x, order, count):
    ids = lax.broadcasted_iota(jnp.int32, (order, count), 0)
    x = list(x)
    for p in range(order):
        pivot = 1.0 / x[p][p : p + 1, :]
        here = ids == p
        row = jnp.where(here, 1.0, x[p])
        for i in range(order):
            if i != p:
                x[i] = jnp.where(here, 0.0, x[i]) - (x[i][p : p + 1, :] * pivot) * row
        x[p] = row * pivot
    return x


def solve_spd(left, right, inverse, count, size):
    for lo in range(0, size, PANEL):
        hi = lo + PANEL
        last = hi == size
        x = [
            jnp.transpose(left[pl.ds(lo + i, count, stride=size), :])[lo:hi, :]
            for i in range(PANEL)
        ]
        x = invert_small(x, PANEL, count)
        rest = jnp.zeros((size - PANEL, count), F32)
        for i in range(PANEL):
            inverse[pl.ds(i, count, stride=PANEL), :] = jnp.transpose(
                jnp.concatenate([x[i], rest], axis=0)
            )
        for item in range(count):
            base = item * size
            rows = slice(base + lo, base + hi)
            panel = right[rows, :]
            if not last:
                panel = jnp.concatenate([left[rows, :], panel], axis=1)
            panel = dot3(inverse[item * PANEL : (item + 1) * PANEL, :PANEL], panel)
            for start, stop in ((0, lo), (hi, size)):
                if start < stop:
                    part = slice(base + start, base + stop)
                    update = dot3(left[part, lo:hi], panel)
                    if not last:
                        left[part, :] -= update[:, :size]
                    right[part, :] -= update[:, -size:]
            if not last:
                left[rows, :] = panel[:, :size]
            right[rows, :] = panel[:, -size:]


def factor_kernel(count, group, tcol, block, basis, high, low, left, right, inverse):
    step = pl.program_id(0)

    @pl.when(tcol[0] == 0)
    def _():
        for g in range(group):
            turned = dot(block[g], basis[g]).astype(BF16)
            rotated = dot_t(basis[g][:, :SPARE], turned)
            corner = rotated[:, :SPARE]
            where = pl.ds(pl.multiple_of((step * group + g) * SPARE, SPARE), SPARE)
            left[where, :] = 0.5 * (corner + jnp.transpose(corner))
            right[where, :] = rotated[:, SPARE:]

        @pl.when(step == pl.num_programs(0) - 1)
        def _():
            solve_spd(left, right, inverse, count, SPARE)
            for item in range(count):
                solved = jnp.transpose(right[item * SPARE : (item + 1) * SPARE, :])
                high[item], low[item] = split(solved)

    @pl.when((tcol[0] != 0) & (step == 0))
    def _():
        high[...] = jnp.zeros_like(high)
        low[...] = jnp.zeros_like(low)


def factor(tcol, near_blocks, bases):
    count = bases.shape[0]
    group = 4
    whole = pl.BlockSpec((count, RANK, SPARE), lambda i: (0, 0, 0))
    shape = jax.ShapeDtypeStruct((count, RANK, SPARE), BF16)
    return pl.pallas_call(
        functools.partial(factor_kernel, count, group),
        grid=(count // group,),
        in_specs=[
            pl.BlockSpec(memory_space=SMEM),
            pl.BlockSpec((group, None, BLK, BLK), lambda i: (i, 0, 0, 0)),
            pl.BlockSpec((group, BLK, BLK), lambda i: (i, 0, 0)),
        ],
        out_specs=[whole, whole],
        out_shape=[shape, shape],
        scratch_shapes=[
            VMEM((count * SPARE, SPARE), F32),
            VMEM((count * SPARE, SPARE), F32),
            VMEM((count * PANEL, SPARE), F32),
        ],
        compiler_params=PARAMS,
        name="factor",
    )(tcol, near_blocks, bases)


def rotate_kernel(slots, group, position, block, basis, partners, upper, lower):
    step = pl.program_id(0)
    for g in range(group):
        turned = jnp.concatenate(
            [
                dot(block[g, k], partners[position[step * group + g, k]]).astype(BF16)
                for k in range(slots)
            ],
            axis=1,
        )
        rotated = dot_t(basis[g], turned)
        upper[g, :SPARE], upper[g, SPARE:] = split(rotated[:SPARE])
        lower[g] = rotated[SPARE:]


def rotate(position, near_blocks, bases, partners):
    count, slots = near_blocks.shape[:2]
    group = 2
    width = slots * RANK
    return pl.pallas_call(
        functools.partial(rotate_kernel, slots, group),
        grid=(count // group,),
        in_specs=[
            pl.BlockSpec(memory_space=SMEM),
            pl.BlockSpec((group, slots, BLK, BLK), lambda i: (i, 0, 0, 0)),
            pl.BlockSpec((group, BLK, BLK), lambda i: (i, 0, 0)),
            pl.BlockSpec(partners.shape, lambda i: (0, 0, 0)),
        ],
        out_specs=[
            pl.BlockSpec((group, 2 * SPARE, width), lambda i: (i, 0, 0)),
            pl.BlockSpec((group, RANK, width), lambda i: (i, 0, 0)),
        ],
        out_shape=[
            jax.ShapeDtypeStruct((count, 2 * SPARE, width), BF16),
            jax.ShapeDtypeStruct((count, RANK, width), F32),
        ],
        compiler_params=PARAMS,
        cost_estimate=pl.CostEstimate(
            flops=4 * count * slots * BLK * BLK * RANK * 2, bytes_accessed=12 << 20, transcendentals=0
        ),
        name="rotate",
    )(position, near_blocks, bases, partners)


def reduce_kernel(slots, group, high, low, upper, lower, skeleton, packed):
    for g in range(group):
        update = dot(jnp.concatenate([high[g], high[g]], axis=1), upper[g])
        update += dot(low[g], upper[g, :SPARE])
        result = lower[g] - update
        for k in range(slots):
            part = result[:, k * RANK : (k + 1) * RANK]
            skeleton[g, k] = part
            packed[g, k] = part.astype(BF16)


def reduce_rows(high, low, upper, lower):
    count, _, width = lower.shape
    slots = width // RANK
    group = 4
    solved = pl.BlockSpec((group, RANK, SPARE), lambda i: (i, 0, 0))
    blocks = pl.BlockSpec((group, slots, RANK, RANK), lambda i: (i, 0, 0, 0))
    shape = (count, slots, RANK, RANK)
    return pl.pallas_call(
        functools.partial(reduce_kernel, slots, group),
        grid=(count // group,),
        in_specs=[
            solved,
            solved,
            pl.BlockSpec((group, 2 * SPARE, width), lambda i: (i, 0, 0)),
            pl.BlockSpec((group, RANK, width), lambda i: (i, 0, 0)),
        ],
        out_specs=[blocks, blocks],
        out_shape=[jax.ShapeDtypeStruct(shape, F32), jax.ShapeDtypeStruct(shape, BF16)],
        compiler_params=PARAMS,
        name="reduce_rows",
    )(high, low, upper, lower)


def upper_kernel(parents, slots, target, blocks, basis, partners, out, merged, left, right, inverse):
    merged[...] = jnp.zeros_like(merged)
    for p in range(parents):
        for a in range(2):
            for k in range(slots):
                merged[p, target[2 * p + a, k], a * RANK : (a + 1) * RANK] = blocks[2 * p + a, k]
    lifted = []
    for p in range(parents):
        mixed = []
        for d in (2, 0, 1, 3, 4):
            pair = jnp.concatenate([merged[p, 2 * d], merged[p, 2 * d + 1]], axis=1)
            partner = basis[p] if d == 2 else partners[p + d]
            mixed.append(dot(pair, partner).astype(BF16))
        result = dot_t(basis[p], jnp.concatenate(mixed, axis=1))
        corner = result[:RANK, :RANK]
        rows = slice(p * RANK, (p + 1) * RANK)
        left[rows, :] = 0.5 * (corner + jnp.transpose(corner))
        right[rows, :] = result[:RANK, RANK : 2 * RANK]
        lifted.append(result[:, RANK:])
    solve_spd(left, right, inverse, parents, RANK)
    for p in range(parents):
        solved = jnp.transpose(right[p * RANK : (p + 1) * RANK, :])
        result = lifted[p][RANK:] - dot3(solved, lifted[p][:RANK])
        for place, d in enumerate((2, 0, 1, 3, 4)):
            out[p, d] = result[:, place * RANK : (place + 1) * RANK]


def upper_level(target, blocks, bases, partners):
    parents = bases.shape[0]
    slots = blocks.shape[1]
    return pl.pallas_call(
        functools.partial(upper_kernel, parents, slots),
        in_specs=[pl.BlockSpec(memory_space=SMEM)] + [pl.BlockSpec(memory_space=VMEM)] * 3,
        out_specs=pl.BlockSpec(memory_space=VMEM),
        out_shape=jax.ShapeDtypeStruct((parents, 5, RANK, RANK), F32),
        scratch_shapes=[
            VMEM((parents, 10, 2 * RANK, RANK), BF16),
            VMEM((parents * RANK, RANK), F32),
            VMEM((parents * RANK, RANK), F32),
            VMEM((parents * PANEL, RANK), F32),
        ],
        compiler_params=PARAMS,
        name="upper_level",
    )(target, blocks, bases, partners)


def per_device(near_blocks, leaf_bases, upper_bases, neighbours):
    leaf_count = near_blocks.shape[0]
    rows = ("node", "trow")
    everyone = ("node", "trow", "tcol")
    leaf_total = leaf_count * lax.axis_size(rows)
    parents_all = leaf_total // 2
    first_leaf = lax.axis_index(rows) * leaf_count
    tcol = lax.axis_index("tcol")
    tcols = lax.axis_size("tcol")
    owned = leaf_count // tcols

    lists = lax.all_to_all(neighbours, "tcol", split_axis=0, concat_axis=1, tiled=True)
    owned_ids = first_leaf + tcol * owned + jnp.arange(owned, dtype=jnp.int32)
    target = 2 * ((lists // 2 - owned_ids[:, None] // 2 + 2) % parents_all) + lists % 2

    own = leaf_bases[:, :, SPARE:]
    before = ring(own[leaf_count - REACH :], rows, 1)
    after = ring(own[:REACH], rows, -1)
    partners = jnp.concatenate([before, own, after], axis=0)
    position = (neighbours - first_leaf + leaf_total // 2) % leaf_total - leaf_total // 2 + REACH

    upper_own = upper_bases[:, :, RANK:]
    upper_partners = jnp.concatenate(
        [ring(upper_own, everyone, 1), upper_own, ring(upper_own, everyone, -1)], axis=0
    )

    high, low = factor(tcol.reshape(1), near_blocks, leaf_bases)
    half = leaf_count // 2
    parts = []
    for part in (high[:half], high[half:]):
        held = part
        for hop in range(tcols - 1):
            got = lax.ppermute(held, "tcol", [(hop, hop + 1)])
            held = jnp.where(tcol == hop + 1, got, held)
        parts.append(held)
    high = jnp.concatenate(parts, axis=0)
    upper, lower = rotate(position, near_blocks, leaf_bases, partners)
    skeleton, packed = reduce_rows(high, low, upper, lower)
    arrived = lax.all_to_all(packed, "tcol", split_axis=0, concat_axis=1, tiled=True)
    upper_skeleton = upper_level(target, arrived, upper_bases, upper_partners)
    return (skeleton, upper_skeleton)


def solution(mesh):
    return jax.shard_map(
        per_device,
        mesh=mesh,
        in_specs=(
            P(("node", "trow"), "tcol", None, None),
            P(("node", "trow"), None, None),
            P(("node", "trow", "tcol"), None, None),
            P(("node", "trow"), "tcol"),
        ),
        out_specs=(
            P(("node", "trow"), "tcol", None, None),
            P(("node", "trow", "tcol"), None, None, None),
        ),
        check_vma=False,
    )
```

time: 1030 us -> 111 us (0.11)
  other arithmetic: 813 us -> 0.6 us
  waiting for transfers between devices: 132 us -> 27.7 us
  Pallas kernels: 0 us -> 40.4 us
  matrix products: 23 us -> 0 us
  local copies, waits for them, and re-layouts: 24.5 us -> 7.8 us
  starting transfers between devices: 18 us -> 33.5 us
  between operations: 14.4 us -> 0.91 us
    another operation x16 -> x0, other arithmetic: 805 us -> none  [the longest x5 416 us: reduce_rows(): lax.linalg.triangular_solve(widened, rotated[..., :spare_size, spare_size...]
    psum x1 -> x0, waiting for transfers between devices: 81.4 us -> none  [spread(): return lax.psum(block, axis)]
    pallas_call x0 -> x4, Pallas kernels: none -> 40.4 us  [the longest x1 20.1 us: factor(): pl.pallas_call(functools.partial(factor_kernel, count, group), grid=(coun...]
    ppermute x4 -> x10, waiting for transfers between devices: 50.7 us -> 20.9 us  [the longest x4 16.3 us: ring(): lax.ppermute(array, axes, [(i, (i + step) % count) for i in range(count)])]
    dot_general x7 -> x0, matrix products: 13.9 us -> none  [the longest x1 4.9 us: per_device(): jnp.einsum('lkab,lkbc->lkac', near_blocks, partner, preferred_element_typ...]
  transfers between devices with their start and end apart: 7 -> 12, of which waited for: 4 -> 4; matrix products, arithmetic and copies ran while one was open for 32% -> 2% of each run, Pallas kernels for 0% -> 8%
where the time goes in v1:
time: 111 us
  Pallas kernels  40.4 us (36%)
  starting transfers between devices  33.5 us (30%)
  waiting for transfers between devices  27.7 us (25%)
  local copies, waits for them, and re-layouts  7.8 us (7%)
    pallas_call x1, Pallas kernels, factor(): pl.pallas_call(functools.partial(factor_kernel, count, group), grid=(coun...  20.1 us
    ppermute x4, waiting for transfers between devices, ring(): lax.ppermute(array, axes, [(i, (i + step) % count) for i in range(count)])  16.3 us
    all_to_all x1, starting transfers between devices, per_device(): lax.all_to_all(packed, 'tcol', split_axis=0, concat_axis=1, tiled=True)  12.7 us
    pallas_call x1, Pallas kernels, upper_level(): pl.pallas_call(functools.partial(upper_kernel, parents, slots), in_specs=...  11.6 us
    ppermute x6, starting transfers between devices, per_device(): got = lax.ppermute(held, 'tcol', [(hop, hop + 1)])  8.88 us
    ppermute x4, starting transfers between devices, ring(): lax.ppermute(array, axes, [(i, (i + step) % count) for i in range(count)])  8.73 us
    all_to_all x1, waiting for transfers between devices, per_device(): lax.all_to_all(packed, 'tcol', split_axis=0, concat_axis=1, tiled=True)  6.83 us
    pallas_call x1, Pallas kernels, rotate(): pl.pallas_call(functools.partial(rotate_kernel, slots, group), grid=(coun...  6.05 us
  transfers between devices with their start and end apart: 12, of which 4 were waited for; matrix products, arithmetic and copies ran while one was open for 2% of the time, Pallas kernels for 8%

profile of v1, /device:TPU:0, one launch (start us, length us, event | category | flops | bytes accessed | tf_op | source)
XLA Modules:
  0.0 110.9 jit_solution(11143911765969388005)
XLA Ops:
  0.6 1.6 %copy-done = bf16[16,256,256]{2,1,0:T(8,128)(2,1)S(1)} copy-done((bf16[16,256,256]{2,1,0:T(8,128)(2,1)S(1)}, bf16[16,256,256]{2,1,0:T(8,128)(2,1)}, u32[]{:S(2)}) %copy-start) | copy-done | bytes 2097176
  2.2 2.2 %copy-done.2 = bf16[16,2,256,256]{3,2,1,0:T(8,128)(2,1)S(1)} copy-done((bf16[16,2,256,256]{3,2,1,0:T(8,128)(2,1)S(1)}, bf16[16,2,256,256]{3,2,1,0:T(8,128)(2,1)}, u32[]{:S(2)}) %copy-start.2) | copy-done | bytes 4194328
  4.4 20.1 %factor.1 = (bf16[16,128,128]{2,1,0:T(8,128)(2,1)S(1)}, bf16[16,128,128]{2,1,0:T(8,128)(2,1)S(1)}) custom-call(s32[1]{0:T(128)} %bitcast.tcol, bf16[16,2,256,256]{3,2,1,0:T(8,128)(2,1)S(1)} %copy-done.2, bf16[16,256,256]{2,1,0:T(8,128)(2,1)S(1)} %copy-done), custom_call_target="tpu_custom_call" | custom-call | tf_op jit(solution)/shard_map/factor/pallas_call | solution.py:127
  24.5 1.3 %collective-permute-start = (bf16[8,128,128]{2,1,0:T(8,128)(2,1)S(1)}, bf16[8,128,128]{2,1,0:T(8,128)(2,1)S(1)}, u32[]{:S(2)}, u32[]{:S(2)}) collective-permute-start(bf16[8,128,128]{2,1,0:T(8,128)(2,1)S(1)} %slice.20), channel_id=1, source_target_pairs={{0,1},{4,5},{8,9},{12,13},{16,17},{20,21},{24,25},{28,29}} | collective-permute-start | bytes 786440 | tf_op jit(solution)/shard_map/ppermute | solution.py:303
  25.8 0.9 fusion.8
  26.7 2.9 %collective-permute-start.6 = (bf16[4,256,128]{2,1,0:T(8,128)(2,1)}, bf16[4,256,128]{2,1,0:T(8,128)(2,1)S(1)}, u32[]{:S(2)}, u32[]{:S(2)}) collective-permute-start(bf16[4,256,128]{2,1,0:T(8,128)(2,1)} %get-tuple-element.14), channel_id=1, source_target_pairs={{0,4},{4,8},{8,12},{12,16},{16,20},{20,24},{24,28},{28,0},{1,5},{5... | collective-permute-start | bytes 786440 | tf_op jit(solution)/shard_map/ppermute | solution.py:24
  29.6 0.4 collective-permute-start.7
  30.0 0.1 all_to_all.27
  30.1 0.6 copy.23
  30.7 3.2 %all-to-all-start = ((s32[4,4,2]{1,2,0:T(2,128)}), s32[4,4,2]{1,2,0:T(2,128)S(1)}, u32[]{:S(2)}, u32[]{:S(2)}) async-start(s32[4,4,2]{1,2,0:T(2,128)} %copy.23), calls=%async_computation | async-start | bytes 8192 | tf_op jit(solution)/shard_map/all_to_all | solution.py:282
  34.0 0.1 broadcast_select_fusion.1
  34.1 4.7 %collective-permute-start.3 = (bf16[8,128,128]{2,1,0:T(8,128)(2,1)S(1)}, bf16[8,128,128]{2,1,0:T(8,128)(2,1)}, u32[]{:S(2)}, u32[]{:S(2)}) collective-permute-start(bf16[8,128,128]{2,1,0:T(8,128)(2,1)S(1)} %get-tuple-element.17), channel_id=1, source_target_pairs={{0,1},{4,5},{8,9},{12,13},{16,17},{20,21},{24,25},{28,29}} | collective-permute-start | bytes 786440 | tf_op jit(solution)/shard_map/ppermute | solution.py:303
  38.8 0.1 copy.22
  38.9 0.7 collective-permute-start.1
  39.6 4.6 %collective-permute-done.3 = bf16[8,128,128]{2,1,0:T(8,128)(2,1)} collective-permute-done((bf16[8,128,128]{2,1,0:T(8,128)(2,1)S(1)}, bf16[8,128,128]{2,1,0:T(8,128)(2,1)}, u32[]{:S(2)}, u32[]{:S(2)}) %collective-permute-start.3) | collective-permute-done | bytes 262176 | tf_op jit(solution)/shard_map/ppermute | solution.py:303
  44.2 0.8 collective-permute-start.4
  45.1 0.2 pad_maximum_fusion.partners
  45.3 0.7 collective-permute-start.2
  46.0 0.7 collective-permute-start.5
  46.7 2.2 %copy-done.3 = bf16[16,2,256,256]{3,2,1,0:T(8,128)(2,1)S(1)} copy-done((bf16[16,2,256,256]{3,2,1,0:T(8,128)(2,1)S(1)}, bf16[16,2,256,256]{3,2,1,0:T(8,128)(2,1)}, u32[]{:S(2)}) %copy-start.3) | copy-done | bytes 4194328
  48.9 6.0 %rotate.1 = (bf16[16,256,256]{2,1,0:T(8,128)(2,1)S(1)}, f32[16,128,256]{2,1,0:T(8,128)S(1)}) custom-call(s32[16,2]{1,0:T(8,128)S(1)} %fusion.1.position, bf16[16,2,256,256]{3,2,1,0:T(8,128)(2,1)S(1)} %copy-done.3, bf16[16,256,256]{2,1,0:T(8,128)(2,1)S(1)} %copy-done.1, bf16[24,256,128]{2,1,0:T(8,128)(2,1)S(1)} %pad_maximum_fusion.partners), custom_call_target="tpu_custom_call" | custom-call | flops 2147483648 | bytes 12582912 | tf_op jit(solution)/shard_map/rotate/pallas_call | solution.py:166
  55.1 2.7 %reduce_rows.1 = (f32[16,2,128,128]{3,2,1,0:T(8,128)}, bf16[16,2,128,128]{3,2,1,0:T(8,128)(2,1)}) custom-call(bf16[16,128,128]{2,1,0:T(8,128)(2,1)S(1)} %pad_maximum_fusion.1.high, bf16[16,128,128]{2,1,0:T(8,128)(2,1)S(1)} %get-tuple-element.9.low, bf16[16,256,256]{2,1,0:T(8,128)(2,1)S(1)} %get-tuple-element.10.upper, ...), custom_call_target="tpu_custom_call" | custom-call | tf_op jit(solution)/shard_map/reduce_rows/pallas_call | solution.py:209
  57.8 12.7 %all-to-all-start.1 = ((bf16[16,2,128,128]{3,2,1,0:T(8,128)(2,1)}), bf16[16,2,128,128]{3,2,1,0:T(8,128)(2,1)S(1)}, u32[]{:S(2)}, u32[]{:S(2)}) async-start(bf16[16,2,128,128]{3,2,1,0:T(8,128)(2,1)} %get-tuple-element.13), calls=%async_computation.1 | async-start | bytes 2097152 | tf_op jit(solution)/shard_map/all_to_all | solution.py:309
  70.5 2.1 %collective-permute-start.8 = (bf16[2,256,128]{2,1,0:T(8,128)(2,1)S(1)}, bf16[2,256,128]{2,1,0:T(8,128)(2,1)S(1)}, u32[]{:S(2)}, u32[]{:S(2)}) collective-permute-start(bf16[2,256,128]{2,1,0:T(8,128)(2,1)S(1)} %slice.25), channel_id=1, source_target_pairs={{0,1},{1,2},{2,3},{3,4},{4,5},{5,6},{6,7},{7,8},{8,9},{9,10},{10,1... | collective-permute-start | bytes 393224 | tf_op jit(solution)/shard_map/ppermute | solution.py:24
  72.6 3.3 %collective-permute-start.9 = (bf16[2,256,128]{2,1,0:T(8,128)(2,1)S(1)}, bf16[2,256,128]{2,1,0:T(8,128)(2,1)S(1)}, u32[]{:S(2)}, u32[]{:S(2)}) collective-permute-start(bf16[2,256,128]{2,1,0:T(8,128)(2,1)S(1)} %slice.25), channel_id=1, source_target_pairs={{0,31},{1,0},{2,1},{3,2},{4,3},{5,4},{6,5},{7,6},{8,7},{9,8},{10,9... | collective-permute-start | bytes 393224 | tf_op jit(solution)/shard_map/ppermute | solution.py:24
  75.9 0.1 copy.24
  76.0 0.1 fusion.6.target
  76.1 14.8 %collective-permute-done.8 = bf16[2,256,128]{2,1,0:T(8,128)(2,1)S(1)} collective-permute-done((bf16[2,256,128]{2,1,0:T(8,128)(2,1)S(1)}, bf16[2,256,128]{2,1,0:T(8,128)(2,1)S(1)}, u32[]{:S(2)}, u32[]{:S(2)}) %collective-permute-start.8) | collective-permute-done | bytes 131104 | tf_op jit(solution)/shard_map/ppermute | solution.py:24
  90.9 1.4 %collective-permute-done.9 = bf16[2,256,128]{2,1,0:T(8,128)(2,1)S(1)} collective-permute-done((bf16[2,256,128]{2,1,0:T(8,128)(2,1)S(1)}, bf16[2,256,128]{2,1,0:T(8,128)(2,1)S(1)}, u32[]{:S(2)}, u32[]{:S(2)}) %collective-permute-start.9) | collective-permute-done | bytes 131104 | tf_op jit(solution)/shard_map/ppermute | solution.py:24
  92.4 6.8 %all-to-all-done.1 = bf16[16,2,128,128]{3,2,1,0:T(8,128)(2,1)S(1)} async-done(((bf16[16,2,128,128]{3,2,1,0:T(8,128)(2,1)}), bf16[16,2,128,128]{3,2,1,0:T(8,128)(2,1)S(1)}, u32[]{:S(2)}, u32[]{:S(2)}) %all-to-all-start.1) | async-done | bytes 1048608 | tf_op jit(solution)/shard_map/all_to_all | solution.py:309
  99.2 0.1 copy.28
  99.3 11.6 %upper_level.1 = f32[2,5,128,128]{3,2,1,0:T(8,128)} custom-call(s32[4,8]{1,0:T(4,128)S(1)} %fusion.6.target, bf16[4,8,128,128]{3,2,1,0:T(8,128)(2,1)S(1)} %bitcast.10, bf16[2,256,256]{2,1,0:T(8,128)(2,1)S(1)} %copy-done.4, bf16[6,256,128]{2,1,0:T(8,128)(2,1)S(1)} %pad_maximum_fusion.2.partners), custom_call_target="tpu_custom_call" | custom-call | tf_op jit(solution)/shard_map/upper_level/pallas_call | solution.py:255
  (31 shorter events, 0.4 us)
Async XLA Ops:
  0.6 1.6 %copy-start = (bf16[16,256,256]{2,1,0:T(8,128)(2,1)S(1)}, bf16[16,256,256]{2,1,0:T(8,128)(2,1)}, u32[]{:S(2)}) copy-start(bf16[16,256,256]{2,1,0:T(8,128)(2,1)} %basis.4) | copy-start | bytes 6291460
  2.2 2.2 %copy-start.2 = (bf16[16,2,256,256]{3,2,1,0:T(8,128)(2,1)S(1)}, bf16[16,2,256,256]{3,2,1,0:T(8,128)(2,1)}, u32[]{:S(2)}) copy-start(bf16[16,2,256,256]{3,2,1,0:T(8,128)(2,1)} %block.3) | copy-start | bytes 12582916
  4.4 25.6 %copy-start.5 = (s32[16,2]{0,1:T(2,128)S(1)}, s32[16,2]{0,1:T(2,128)}, u32[]{:S(2)}) copy-start(s32[16,2]{0,1:T(2,128)} %param.7) | copy-start | bytes 388
  24.5 9.5 %collective-permute-start = (bf16[8,128,128]{2,1,0:T(8,128)(2,1)S(1)}, bf16[8,128,128]{2,1,0:T(8,128)(2,1)S(1)}, u32[]{:S(2)}, u32[]{:S(2)}) collective-permute-start(bf16[8,128,128]{2,1,0:T(8,128)(2,1)S(1)} %slice.20), channel_id=1, source_target_pairs={{0,1},{4,5},{8,9},{12,13},{16,17},{20,21},{24,25},{28,29}} | collective-permute-start | bytes 786440 | tf_op jit(solution)/shard_map/ppermute | solution.py:303
  26.7 18.3 %collective-permute-start.6 = (bf16[4,256,128]{2,1,0:T(8,128)(2,1)}, bf16[4,256,128]{2,1,0:T(8,128)(2,1)S(1)}, u32[]{:S(2)}, u32[]{:S(2)}) collective-permute-start(bf16[4,256,128]{2,1,0:T(8,128)(2,1)} %get-tuple-element.14), channel_id=1, source_target_pairs={{0,4},{4,8},{8,12},{12,16},{16,20},{20,24},{24,28},{28,0},{1,5},{5... | collective-permute-start | bytes 786440 | tf_op jit(solution)/shard_map/ppermute | solution.py:24
  29.6 15.4 %collective-permute-start.7 = (bf16[4,256,128]{2,1,0:T(8,128)(2,1)}, bf16[4,256,128]{2,1,0:T(8,128)(2,1)S(1)}, u32[]{:S(2)}, u32[]{:S(2)}) collective-permute-start(bf16[4,256,128]{2,1,0:T(8,128)(2,1)} %get-tuple-element.15), channel_id=1, source_target_pairs={{0,28},{4,0},{8,4},{12,8},{16,12},{20,16},{24,20},{28,24},{1,29},{... | collective-permute-start | bytes 786440 | tf_op jit(solution)/shard_map/ppermute | solution.py:24
  30.7 27.1 %all-to-all-start = ((s32[4,4,2]{1,2,0:T(2,128)}), s32[4,4,2]{1,2,0:T(2,128)S(1)}, u32[]{:S(2)}, u32[]{:S(2)}) async-start(s32[4,4,2]{1,2,0:T(2,128)} %copy.23), calls=%async_computation | async-start | bytes 8192 | tf_op jit(solution)/shard_map/all_to_all | solution.py:282
  34.0 11.1 %slice-start = ((bf16[16,256,256]{2,1,0:T(8,128)(2,1)}), bf16[16,256,128]{2,1,0:T(8,128)(2,1)S(1)}, s32[]{:S(2)}) async-start(bf16[16,256,256]{2,1,0:T(8,128)(2,1)} %basis.4), calls=%async_computation.2 | async-start | bytes 2097152 | tf_op jit(solution)/shard_map/slice | solution.py:286
  34.1 10.1 %collective-permute-start.3 = (bf16[8,128,128]{2,1,0:T(8,128)(2,1)S(1)}, bf16[8,128,128]{2,1,0:T(8,128)(2,1)}, u32[]{:S(2)}, u32[]{:S(2)}) collective-permute-start(bf16[8,128,128]{2,1,0:T(8,128)(2,1)S(1)} %get-tuple-element.17), channel_id=1, source_target_pairs={{0,1},{4,5},{8,9},{12,13},{16,17},{20,21},{24,25},{28,29}} | collective-permute-start | bytes 786440 | tf_op jit(solution)/shard_map/ppermute | solution.py:303
  38.9 6.4 %collective-permute-start.1 = (bf16[8,128,128]{2,1,0:T(8,128)(2,1)S(1)}, bf16[8,128,128]{2,1,0:T(8,128)(2,1)S(1)}, u32[]{:S(2)}, u32[]{:S(2)}) collective-permute-start(bf16[8,128,128]{2,1,0:T(8,128)(2,1)S(1)} %get-tuple-element.16), channel_id=1, source_target_pairs={{1,2},{5,6},{9,10},{13,14},{17,18},{21,22},{25,26},{29,30}} | collective-permute-start | bytes 786440 | tf_op jit(solution)/shard_map/ppermute | solution.py:303
  44.2 2.5 %copy-start.1 = (bf16[16,256,256]{2,1,0:T(8,128)(2,1)S(1)}, bf16[16,256,256]{2,1,0:T(8,128)(2,1)}, u32[]{:S(2)}) copy-start(bf16[16,256,256]{2,1,0:T(8,128)(2,1)} %basis.4) | copy-start | bytes 6291460
  44.2 1.8 %collective-permute-start.4 = (bf16[8,128,128]{2,1,0:T(8,128)(2,1)S(1)}, bf16[8,128,128]{2,1,0:T(8,128)(2,1)S(1)}, u32[]{:S(2)}, u32[]{:S(2)}) collective-permute-start(bf16[8,128,128]{2,1,0:T(8,128)(2,1)S(1)} %broadcast_select_fusion), channel_id=1, source_target_pairs={{1,2},{5,6},{9,10},{13,14},{17,18},{21,22},{25,26},{29,30}} | collective-permute-start | bytes 786440 | tf_op jit(solution)/shard_map/ppermute | solution.py:303
  45.3 9.7 %collective-permute-start.2 = (bf16[8,128,128]{2,1,0:T(8,128)(2,1)S(1)}, bf16[8,128,128]{2,1,0:T(8,128)(2,1)S(1)}, u32[]{:S(2)}, u32[]{:S(2)}) collective-permute-start(bf16[8,128,128]{2,1,0:T(8,128)(2,1)S(1)} %broadcast_select_fusion.3), channel_id=1, source_target_pairs={{2,3},{6,7},{10,11},{14,15},{18,19},{22,23},{26,27},{30,31}} | collective-permute-start | bytes 786440 | tf_op jit(solution)/shard_map/ppermute | solution.py:303
  46.0 9.0 %collective-permute-start.5 = (bf16[8,128,128]{2,1,0:T(8,128)(2,1)S(1)}, bf16[8,128,128]{2,1,0:T(8,128)(2,1)S(1)}, u32[]{:S(2)}, u32[]{:S(2)}) collective-permute-start(bf16[8,128,128]{2,1,0:T(8,128)(2,1)S(1)} %broadcast_select_fusion.2), channel_id=1, source_target_pairs={{2,3},{6,7},{10,11},{14,15},{18,19},{22,23},{26,27},{30,31}} | collective-permute-start | bytes 786440 | tf_op jit(solution)/shard_map/ppermute | solution.py:303
  46.7 2.2 %copy-start.3 = (bf16[16,2,256,256]{3,2,1,0:T(8,128)(2,1)S(1)}, bf16[16,2,256,256]{3,2,1,0:T(8,128)(2,1)}, u32[]{:S(2)}) copy-start(bf16[16,2,256,256]{3,2,1,0:T(8,128)(2,1)} %block.3) | copy-start | bytes 12582916
  57.8 12.7 %copy-start.4 = (bf16[2,256,256]{2,1,0:T(8,128)(2,1)S(1)}, bf16[2,256,256]{2,1,0:T(8,128)(2,1)}, u32[]{:S(2)}) copy-start(bf16[2,256,256]{2,1,0:T(8,128)(2,1)} %basis.5) | copy-start | bytes 786436
  57.8 41.4 %all-to-all-start.1 = ((bf16[16,2,128,128]{3,2,1,0:T(8,128)(2,1)}), bf16[16,2,128,128]{3,2,1,0:T(8,128)(2,1)S(1)}, u32[]{:S(2)}, u32[]{:S(2)}) async-start(bf16[16,2,128,128]{3,2,1,0:T(8,128)(2,1)} %get-tuple-element.13), calls=%async_computation.1 | async-start | bytes 2097152 | tf_op jit(solution)/shard_map/all_to_all | solution.py:309
  70.5 20.4 %collective-permute-start.8 = (bf16[2,256,128]{2,1,0:T(8,128)(2,1)S(1)}, bf16[2,256,128]{2,1,0:T(8,128)(2,1)S(1)}, u32[]{:S(2)}, u32[]{:S(2)}) collective-permute-start(bf16[2,256,128]{2,1,0:T(8,128)(2,1)S(1)} %slice.25), channel_id=1, source_target_pairs={{0,1},{1,2},{2,3},{3,4},{4,5},{5,6},{6,7},{7,8},{8,9},{9,10},{10,1... | collective-permute-start | bytes 393224 | tf_op jit(solution)/shard_map/ppermute | solution.py:24
  72.6 19.8 %collective-permute-start.9 = (bf16[2,256,128]{2,1,0:T(8,128)(2,1)S(1)}, bf16[2,256,128]{2,1,0:T(8,128)(2,1)S(1)}, u32[]{:S(2)}, u32[]{:S(2)}) collective-permute-start(bf16[2,256,128]{2,1,0:T(8,128)(2,1)S(1)} %slice.25), channel_id=1, source_target_pairs={{0,31},{1,0},{2,1},{3,2},{4,3},{5,4},{6,5},{7,6},{8,7},{9,8},{10,9... | collective-permute-start | bytes 393224 | tf_op jit(solution)/shard_map/ppermute | solution.py:24

commit v2 on v0

v2 whole, which is shorter than its diff:
```python
import functools

import jax
import jax.numpy as jnp
from jax import lax
from jax.experimental import pallas as pl
from jax.experimental.pallas import tpu as pltpu
from jax.sharding import PartitionSpec as P

BLK = 256
RANK = 128
SPARE = BLK - RANK
REACH = 4
LEAF_PANEL = 64
UPPER_PANEL = 32
LANES = 128
SUB = 8
ITEMS = LANES // SUB
F32 = jnp.float32
BF16 = jnp.bfloat16
VMEM = pltpu.VMEM
SMEM = pltpu.SMEM
PARAMS = pltpu.CompilerParams(vmem_limit_bytes=24 << 20)
TAIL = 16
WHOLE = pl.BlockSpec(memory_space=VMEM)


def ring(array, axes, step, skip=None):
    count = lax.axis_size(axes)
    if skip is None:
        return lax.ppermute(array, axes, [(i, (i + step) % count) for i in range(count)])
    last = lax.axis_size(skip)
    pairs = [
        (i * last + j, (i + step) % count * last + j) for i in range(count) for j in range(1, last)
    ]
    return lax.ppermute(array, axes + (skip,), pairs)


def hbm(x):
    return pltpu.with_memory_space_constraint(x, pltpu.HBM)


def after(x, *others):
    return lax.optimization_barrier((x, *others))[0]


def split(x):
    high = x.astype(BF16)
    return high, (x - high.astype(F32)).astype(BF16)


def dot(a, b):
    return jnp.dot(a, b, preferred_element_type=F32)


def dot_t(a, b):
    return lax.dot_general(a, b, (((0,), (0,)), ((), ())), preferred_element_type=F32)


def dot3(a, b):
    a_high, a_low = split(a)
    b_high, b_low = split(b)
    return dot(
        jnp.concatenate([a_high, a_high, a_low], axis=1),
        jnp.concatenate([b_high, b_low, b_high], axis=0),
    )


def invert_packed(x, order):
    ids = lax.broadcasted_iota(jnp.int32, (order, LANES), 0)
    lane = lax.broadcasted_iota(jnp.int32, (order, LANES), 1)
    item, place = lane % ITEMS, lane // ITEMS
    x = list(x)
    for g in range(order // SUB):
        rows = [jnp.take_along_axis(x[g], item + c * ITEMS, axis=1) for c in range(SUB)]
        for c in range(SUB):
            p = g * SUB + c
            pivot = 1.0 / rows[c][p : p + 1, :]
            here = ids == p
            row = jnp.where(here, 1.0, rows[c])
            for e in range(SUB):
                if e != c:
                    factor_e = rows[e][p : p + 1, :] * pivot
                    rows[e] = jnp.where(here, 0.0, rows[e]) - factor_e * row
            rows[c] = row * pivot
            for h in range(order // SUB):
                if h != g:
                    factor_h = x[h][p : p + 1, :] * pivot
                    x[h] = jnp.where(here, 0.0, x[h]) - factor_h * row
        joined = rows[0]
        for c in range(1, SUB):
            joined = jnp.where(place == c, rows[c], joined)
        x[g] = joined
    return x


def solve_scratch(count, size, panel):
    return [
        VMEM((ITEMS * size, size), F32),
        VMEM((count * size, size), F32),
        VMEM((ITEMS * panel, LANES), F32),
    ]


def solve_spd(left, right, inverse, count, size, order):
    for lo in range(0, size, order):
        hi = lo + order
        last = hi == size
        x = []
        for g in range(order // SUB):
            rows = [left[pl.ds(lo + g * SUB + c, ITEMS, stride=size), :] for c in range(SUB)]
            x.append(jnp.transpose(jnp.concatenate(rows, axis=0))[lo:hi, :])
        x = invert_packed(x, order)
        rest = jnp.zeros((LANES - order, LANES), F32)
        for g in range(order // SUB):
            rows = jnp.transpose(jnp.concatenate([x[g], rest], axis=0))
            for c in range(SUB):
                inverse[pl.ds(g * SUB + c, ITEMS, stride=order), :] = rows[
                    c * ITEMS : (c + 1) * ITEMS, :
                ]
        for item in range(count):
            base = item * size
            rows = slice(base + lo, base + hi)
            panel = right[rows, :]
            if not last:
                panel = jnp.concatenate([left[rows, :], panel], axis=1)
            panel = dot3(inverse[item * order : (item + 1) * order, :order], panel)
            for start, stop in ((0, lo), (hi, size)):
                if start < stop:
                    part = slice(base + start, base + stop)
                    update = dot3(left[part, lo:hi], panel)
                    if not last:
                        left[part, :] -= update[:, :size]
                    right[part, :] -= update[:, -size:]
            if not last:
                left[rows, :] = panel[:, :size]
            right[rows, :] = panel[:, -size:]


def ends_kernel(basis, first, last):
    for end, when in ((first, 0), (last, pl.num_programs(0) - 1)):

        @pl.when(pl.program_id(0) == when)
        def _():
            end[...] = basis[...]


def ends_of(bases):
    count = bases.shape[0]
    shape = (REACH, BLK, RANK)
    return pl.pallas_call(
        ends_kernel,
        grid=(2,),
        in_specs=[pl.BlockSpec(shape, lambda i: (i * (count // REACH - 1), 0, SPARE // RANK))],
        out_specs=[WHOLE] * 2,
        out_shape=[jax.ShapeDtypeStruct(shape, BF16)] * 2,
        compiler_params=PARAMS,
        name="ends",
    )(bases)


def factor_kernel(count, group, owned, tcol, block, basis, *refs):
    outs, (left, right, inverse) = refs[:4], refs[4:]
    step = pl.program_id(0)
    half = owned // 2

    @pl.when(tcol[0] == 0)
    def _():
        for g in range(group):
            turned = dot(block[g], basis[g]).astype(BF16)
            rotated = dot_t(basis[g][:, :SPARE], turned)
            corner = rotated[:, :SPARE]
            where = pl.ds(pl.multiple_of((step * group + g) * SPARE, SPARE), SPARE)
            left[where, :] = 0.5 * (corner + jnp.transpose(corner))
            right[where, :] = rotated[:, SPARE:]

        @pl.when(step == pl.num_programs(0) - 1)
        def _():
            solve_spd(left, right, inverse, count, SPARE, LEAF_PANEL)
            for item in range(count):
                solved = jnp.transpose(right[item * SPARE : (item + 1) * SPARE, :])
                part = item % owned // half
                place = item // owned * half + item % half
                outs[2 * part][place], outs[2 * part + 1][place] = split(solved)

def factor(tcol, near_blocks, bases, owned):
    count = bases.shape[0]
    group = REACH
    half = count // 2
    steps = count // group
    near = lambda i, t: (jnp.where(t[0] == 0, i, 0), 0, 0, 0)
    basis = lambda i, t: (jnp.where(t[0] == 0, i, 0), 0, 0)
    return pl.pallas_call(
        functools.partial(factor_kernel, count, group, owned),
        grid_spec=pltpu.PrefetchScalarGridSpec(
            num_scalar_prefetch=1,
            grid=(steps,),
            in_specs=[
                pl.BlockSpec((group, None, BLK, BLK), near),
                pl.BlockSpec((group, BLK, BLK), basis),
            ],
            out_specs=[WHOLE, pl.BlockSpec((half, RANK, SPARE), lambda i, t: (0, 0, 0))] * 2,
            scratch_shapes=solve_scratch(count, SPARE, LEAF_PANEL),
        ),
        out_shape=[
            jax.ShapeDtypeStruct((half, RANK, SPARE), BF16),
            pltpu.HBM((half, RANK, SPARE), BF16),
        ]
        * 2,
        compiler_params=PARAMS,
        name="factor",
    )(tcol, near_blocks, bases)


def rotate_kernel(slots, owned, position, block, basis, own, before, later, *refs):
    outs, partners = refs[:4], refs[4]
    step = pl.program_id(0)
    count = own.shape[0]
    half = owned // 2

    @pl.when(step == 0)
    def _():
        partners[:REACH] = before[...]
        partners[REACH : REACH + count] = own[...]
        partners[REACH + count :] = later[...]

    for g in range(owned):
        turned = jnp.concatenate(
            [
                dot(block[g, k], partners[position[step * owned + g, k]]).astype(BF16)
                for k in range(slots)
            ],
            axis=1,
        )
        rotated = dot_t(basis[g], turned)
        upper, lower = outs[g // half * 2 : g // half * 2 + 2]
        place = step * half + g % half
        upper[place, :SPARE], upper[place, SPARE:] = split(rotated[:SPARE])
        lower[g % half] = rotated[SPARE:]


def rotate(position, near_blocks, bases, before, later, owned):
    count, slots = near_blocks.shape[:2]
    half = count // 2
    width = slots * RANK
    ends = pl.BlockSpec(before.shape, lambda i: (0, 0, 0))
    return pl.pallas_call(
        functools.partial(rotate_kernel, slots, owned),
        grid=(count // owned,),
        in_specs=[
            pl.BlockSpec(memory_space=SMEM),
            pl.BlockSpec((owned, slots, BLK, BLK), lambda i: (i, 0, 0, 0)),
            pl.BlockSpec((owned, BLK, BLK), lambda i: (i, 0, 0)),
            pl.BlockSpec((count, BLK, RANK), lambda i: (0, 0, SPARE // RANK)),
            ends,
            ends,
        ],
        out_specs=[WHOLE, pl.BlockSpec((owned // 2, RANK, width), lambda i: (i, 0, 0))] * 2,
        out_shape=[
            jax.ShapeDtypeStruct((half, 2 * SPARE, width), BF16),
            pltpu.HBM((half, RANK, width), F32),
        ]
        * 2,
        scratch_shapes=[VMEM((count + 2 * REACH, BLK, RANK), BF16)],
        compiler_params=PARAMS,
        name="rotate",
    )(position, near_blocks, bases, bases, before, later)


def schur(high, low, upper, lower):
    result = lower - dot(jnp.concatenate([high, high], axis=1), upper)
    return result if low is None else result - dot(low, upper[:SPARE])


def reduce_kernel(part, slots, half, places, tcol, target, *refs):
    tcols = len(places)
    highs, (low, upper, lower) = refs[:tcols], refs[tcols : tcols + 3]
    skeleton, rings = refs[-1 - tcols], refs[-tcols:]
    if part == 0:
        bases = refs[tcols + 3]
        parents, order, _ = bases.shape
        for ring_ref in (rings[1], rings[-1]):
            for p in range(parents):
                at = half * slots * RANK + TAIL + p * order
                ring_ref[at : at + order] = bases[p, :, RANK:]

    def fill(high, low):
        row = lax.broadcasted_iota(jnp.int32, (TAIL, RANK), 0)
        for step in range(tcols):
            owner = lax.rem(tcol[0] + step, tcols)
            marks = jnp.zeros((TAIL, RANK), F32)
            for g in range(half):
                leaf = owner * half + g
                result = schur(
                    high[leaf], None if low is None else low[leaf], upper[leaf], lower[leaf]
                )
                for k in range(slots):
                    at = g * slots + k
                    block = result[:, k * RANK : (k + 1) * RANK]
                    skeleton[owner, 0, g, k] = block
                    rings[step][at * RANK : (at + 1) * RANK] = block.astype(BF16)
                    mark = target[(2 * owner + part) * half + g, k].astype(F32)
                    marks = jnp.where(row == at, mark, marks)
            at = half * slots * RANK
            rings[step][at : at + TAIL] = marks.astype(BF16)

    for high, at in zip(highs, places):

        @pl.when(tcol[0] == at)
        def _():
            fill(high, low if at == 0 else None)


def reduce_rows(part, tcol, target, places, highs, low, upper, lower, bases, skeleton):
    half_count, _, width = lower.shape
    slots = width // RANK
    tcols = len(highs)
    half = half_count // tcols
    const = lambda x: pl.BlockSpec(x.shape, lambda i: (0,) * x.ndim)
    operands = [tcol, target, *highs, hbm(low), upper, hbm(lower)]
    in_specs = [pl.BlockSpec(memory_space=SMEM)] * 2 + [WHOLE] * tcols
    in_specs += [const(low), WHOLE, const(lower)]
    rows = half * slots * RANK + TAIL
    lengths = [rows] * tcols
    if part == 0:
        operands.append(bases)
        in_specs.append(const(bases))
        for k in (1, tcols - 1):
            lengths[k] = rows + bases.shape[0] * bases.shape[1]
    aliases = {}
    if skeleton is not None:
        aliases = {len(operands): 0}
        operands.append(skeleton)
        in_specs.append(pl.BlockSpec(memory_space=pl.ANY))
    return pl.pallas_call(
        functools.partial(reduce_kernel, part, slots, half, places),
        grid=(1,),
        in_specs=in_specs,
        out_specs=[
            pl.BlockSpec(
                (tcols, 1, half, slots, RANK, RANK), lambda i: (0, part, 0, 0, 0, 0)
            )
        ]
        + [WHOLE] * tcols,
        out_shape=[jax.ShapeDtypeStruct((tcols, 2, half, slots, RANK, RANK), F32)]
        + [jax.ShapeDtypeStruct((length, RANK), BF16) for length in lengths],
        input_output_aliases=aliases,
        compiler_params=PARAMS,
        name="reduce_rows",
    )(*operands)


def upper_kernel(parent, parents, tcols, slots, tcol, *refs):
    arrivals, (before, later, edge, basis) = refs[:tcols], refs[tcols : tcols + 4]
    out, merged, left, right, inverse = refs[-5:]
    merged[...] = jnp.zeros_like(merged)
    end = 2 * slots * RANK + TAIL
    for arrival in arrivals:
        marks = arrival[end - TAIL : end].astype(F32)
        for a in range(2):
            for j in range(slots):
                at = a * slots + j
                place = marks[at, 0].astype(jnp.int32)
                merged[place, a * RANK : (a + 1) * RANK] = arrival[at * RANK : (at + 1) * RANK]

    def partner(place):
        if 0 <= place < parents:
            return basis[place, :, RANK:]
        beside, outer = (before, 0) if place < 0 else (later, tcols - 1)
        at = place % parents
        rows = slice(end + at * 2 * RANK, end + (at + 1) * 2 * RANK)
        return jnp.where(tcol[0] == outer, edge[at], beside[rows])

    mixed = []
    for d in (2, 0, 1, 3, 4):
        pair = jnp.concatenate([merged[2 * d], merged[2 * d + 1]], axis=1)
        other = basis[parent] if d == 2 else partner(parent + d - 2)
        mixed.append(dot(pair, other).astype(BF16))
    lifted = dot_t(basis[parent], jnp.concatenate(mixed, axis=1))
    corner = lifted[:RANK, :RANK]
    left[:RANK, :] = 0.5 * (corner + jnp.transpose(corner))
    right[...] = lifted[:RANK, RANK : 2 * RANK]
    solve_spd(left, right, inverse, 1, RANK, UPPER_PANEL)
    result = lifted[RANK:, RANK:] - dot3(jnp.transpose(right[...]), lifted[:RANK, RANK:])
    for place, d in enumerate((2, 0, 1, 3, 4)):
        out[0, d] = result[:, place * RANK : (place + 1) * RANK]


def upper_level(parent, slots, tcol, arrivals, beside, bases, result):
    parents = bases.shape[0]
    operands = [tcol, *arrivals, *beside, bases]
    in_specs = [pl.BlockSpec(memory_space=SMEM)] + [WHOLE] * (len(operands) - 1)
    aliases = {}
    if result is not None:
        aliases = {len(operands): 0}
        operands.append(result)
        in_specs.append(pl.BlockSpec(memory_space=pl.ANY))
    return pl.pallas_call(
        functools.partial(upper_kernel, parent, parents, len(arrivals), slots),
        grid=(1,),
        in_specs=in_specs,
        out_specs=pl.BlockSpec((1, 5, RANK, RANK), lambda i: (parent, 0, 0, 0)),
        out_shape=jax.ShapeDtypeStruct((parents, 5, RANK, RANK), F32),
        input_output_aliases=aliases,
        scratch_shapes=[VMEM((10, 2 * RANK, RANK), BF16)] + solve_scratch(1, RANK, UPPER_PANEL),
        compiler_params=PARAMS,
        name="upper_level",
    )(*operands)


def per_device(near_blocks, leaf_bases, upper_bases, neighbours):
    leaf_count = near_blocks.shape[0]
    rows = ("node", "trow")
    everyone = ("node", "trow", "tcol")
    leaf_total = leaf_count * lax.axis_size(rows)
    parents_all = leaf_total // 2
    first_leaf = lax.axis_index(rows) * leaf_count
    place = lax.axis_index("tcol")
    tcol = place.reshape(1)
    tcols = lax.axis_size("tcol")
    owned = leaf_count // tcols

    leaf_ids = first_leaf + jnp.arange(leaf_count, dtype=jnp.int32)
    position = (neighbours - first_leaf + leaf_total // 2) % leaf_total - leaf_total // 2 + REACH
    target = 2 * ((neighbours // 2 - leaf_ids[:, None] // 2 + 2) % parents_all) + neighbours % 2

    near_blocks, leaf_bases = hbm(near_blocks), hbm(leaf_bases)
    first_ends, last_ends = ends_of(leaf_bases)
    before = ring(last_ends, rows, 1, "tcol")
    later = ring(first_ends, rows, -1, "tcol")
    solved = factor(tcol, near_blocks, leaf_bases, owned)

    relay = tcols // 2
    send = lambda array, start, stop: lax.ppermute(array, "tcol", [(start, stop)])
    halves = (solved[0], solved[2])
    middle = [send(array, 0, relay) for array in halves]
    parts = rotate(position, near_blocks, leaf_bases, before, later, owned)
    places = [0, relay, *range(relay + 1, tcols), *range(relay - 1, 0, -1)]
    highs = []
    for local, got in zip(halves, middle):
        got = after(got, *parts)
        held = [local, got]
        for way, stop in ((1, tcols), (-1, 0)):
            array = got
            for at in range(relay + way, stop, way):
                array = send(array, at - way, at)
                held.append(array)
        highs.append(held)

    pairs = []
    for group in range(lax.axis_size(rows)):
        last, first = group * tcols + tcols - 1, (group + 1) * tcols
        first %= lax.axis_size(everyone)
        pairs += [(last, first), (first, last)]
    edge = lax.ppermute(after(upper_bases, *parts)[:, :, RANK:], everyone, pairs)

    skeleton = None
    arrivals = []
    for part in range(2):
        skeleton, *rings = reduce_rows(
            part,
            tcol,
            target,
            tuple(places),
            highs[part],
            solved[2 * part + 1],
            parts[2 * part],
            parts[2 * part + 1],
            upper_bases,
            skeleton,
        )
        arrivals.append(rings[:1])
        for k in range(1, tcols):
            arrivals[part].append(ring(rings[k], ("tcol",), k))

    beside = (arrivals[0][1], arrivals[0][-1], edge)
    result = None
    for part in range(2):
        result = upper_level(
            part, near_blocks.shape[1], tcol, arrivals[part], beside, upper_bases, result
        )
    skeleton = skeleton.reshape((leaf_count,) + skeleton.shape[3:])
    return (skeleton, result)


def solution(mesh):
    return jax.shard_map(
        per_device,
        mesh=mesh,
        in_specs=(
            P(("node", "trow"), "tcol", None, None),
            P(("node", "trow"), None, None),
            P(("node", "trow", "tcol"), None, None),
            P(("node", "trow"), "tcol"),
        ),
        out_specs=(
            P(("node", "trow"), "tcol", None, None),
            P(("node", "trow", "tcol"), None, None, None),
        ),
        check_vma=False,
    )
```

time: 1030 us -> 85.6 us (0.08)
  other arithmetic: 813 us -> 0.12 us
  waiting for transfers between devices: 132 us -> 14 us
  Pallas kernels: 0 us -> 44.5 us
  local copies, waits for them, and re-layouts: 24.5 us -> 0.19 us
  matrix products: 23 us -> 0 us
  between operations: 14.4 us -> 0.81 us
    another operation x16 -> x0, other arithmetic: 805 us -> none  [the longest x5 416 us: reduce_rows(): lax.linalg.triangular_solve(widened, rotated[..., :spare_size, spare_size...]
    psum x1 -> x0, waiting for transfers between devices: 81.4 us -> none  [spread(): return lax.psum(block, axis)]
    pallas_call x0 -> x7, Pallas kernels: none -> 44.5 us  [the longest x1 15.2 us: factor(): pl.pallas_call(functools.partial(factor_kernel, count, group, owned), gri...]
    ppermute x4 -> x15, waiting for transfers between devices: 50.7 us -> 14 us  [the longest x6 13.6 us: ring(): lax.ppermute(array, axes, [(i, (i + step) % count) for i in range(count)])]
    ppermute x4 -> x15, starting transfers between devices: 8.86 us -> 25 us  [the longest x6 13.3 us: ring(): lax.ppermute(array, axes, [(i, (i + step) % count) for i in range(count)])]
    dot_general x7 -> x0, matrix products: 13.9 us -> none  [the longest x1 4.9 us: per_device(): jnp.einsum('lkab,lkbc->lkac', near_blocks, partner, preferred_element_typ...]
  transfers between devices with their start and end apart: 7 -> 15, of which waited for: 4 -> 4; matrix products, arithmetic and copies ran while one was open for 32% -> 0% of each run, Pallas kernels for 0% -> 43%
where the time goes in v2:
time: 85.6 us; the launch traced here: 84.5 us
  Pallas kernels  44.5 us (52%)
  starting transfers between devices  25 us (29%)
  waiting for transfers between devices  14 us (16%)
    pallas_call x1, Pallas kernels, factor(): pl.pallas_call(functools.partial(factor_kernel, count, group, owned), gri...  15.2 us
    pallas_call x2, Pallas kernels, upper_level(): pl.pallas_call(functools.partial(upper_kernel, parent, parents, len(arriv...  14.5 us
    ppermute x6, waiting for transfers between devices, ring(): lax.ppermute(array, axes, [(i, (i + step) % count) for i in range(count)])  13.6 us
    ppermute x6, starting transfers between devices, ring(): lax.ppermute(array, axes, [(i, (i + step) % count) for i in range(count)])  13.3 us
    pallas_call x1, Pallas kernels, rotate(): pl.pallas_call(functools.partial(rotate_kernel, slots, owned), grid=(coun...  7.68 us
    ppermute x6, starting transfers between devices, per_device(): lax.ppermute(array, 'tcol', [(start, stop)])  6.66 us
    pallas_call x2, Pallas kernels, reduce_rows(): pl.pallas_call(functools.partial(reduce_kernel, part, slots, half, places...  5.99 us
    ppermute x1, starting transfers between devices, per_device(): lax.ppermute(after(upper_bases, *parts)[:, :, RANK:], everyone, pairs)  3.6 us
  transfers between devices with their start and end apart: 15, of which 4 were waited for; matrix products, arithmetic and copies ran while one was open for 0% of the time, Pallas kernels for 43%

profile of v2, /device:TPU:0, one launch (start us, length us, event | category | flops | bytes accessed | tf_op | source)
XLA Modules:
  0.0 84.5 jit_solution(2504772316346473217)
XLA Ops:
  0.6 1.1 %ends.1 = (bf16[4,256,128]{2,1,0:T(8,128)(2,1)S(1)}, bf16[4,256,128]{2,1,0:T(8,128)(2,1)S(1)}) custom-call(bf16[16,256,256]{2,1,0:T(8,128)(2,1)} %own.1), custom_call_target="tpu_custom_call" | custom-call | tf_op jit(solution)/shard_map/ends/pallas_call | solution.py:151
  1.7 0.7 collective-permute-start.1
  2.4 0.7 collective-permute-start.2
  3.1 0.0 copy-start.1
  3.1 15.2 %factor.1 = (bf16[8,128,128]{2,1,0:T(8,128)(2,1)}, bf16[8,128,128]{2,1,0:T(8,128)(2,1)}, bf16[8,128,128]{2,1,0:T(8,128)(2,1)S(1)}, bf16[8,128,128]{2,1,0:T(8,128)(2,1)}) custom-call(s32[1]{0:T(128)} %bitcast.tcol, bf16[16,2,256,256]{3,2,1,0:T(8,128)(2,1)} %block.3, bf16[16,256,256]{2,1,0:T(8,128)(2,1)} %own.1), custom_call_target="tpu_custom_call" | custom-call | tf_op jit(solution)/shard_map/factor/pallas_call | solution.py:193
  18.3 2.0 %collective-permute-start.5 = (bf16[8,128,128]{2,1,0:T(8,128)(2,1)}, bf16[8,128,128]{2,1,0:T(8,128)(2,1)}, u32[]{:S(2)}, u32[]{:S(2)}) collective-permute-start(bf16[8,128,128]{2,1,0:T(8,128)(2,1)} %get-tuple-element.34.refs_0_), channel_id=1, source_target_pairs={{0,2},{4,6},{8,10},{12,14},{16,18},{20,22},{24,26},{28,30}} | collective-permute-start | bytes 786440 | tf_op jit(solution)/shard_map/ppermute | solution.py:434
  20.3 1.3 %collective-permute-start = (bf16[8,128,128]{2,1,0:T(8,128)(2,1)S(1)}, bf16[8,128,128]{2,1,0:T(8,128)(2,1)S(1)}, u32[]{:S(2)}, u32[]{:S(2)}) collective-permute-start(bf16[8,128,128]{2,1,0:T(8,128)(2,1)S(1)} %get-tuple-element.25.refs_0_), channel_id=1, source_target_pairs={{0,2},{4,6},{8,10},{12,14},{16,18},{20,22},{24,26},{28,30}} | collective-permute-start | bytes 786440 | tf_op jit(solution)/shard_map/ppermute | solution.py:434
  21.6 0.1 copy.18
  21.8 0.0 collective-permute-done.2.later
  21.8 7.7 %rotate.1 = (bf16[8,256,256]{2,1,0:T(8,128)(2,1)S(1)}, f32[8,128,256]{2,1,0:T(8,128)}, bf16[8,256,256]{2,1,0:T(8,128)(2,1)S(1)}, f32[8,128,256]{2,1,0:T(8,128)}) custom-call(s32[16,2]{1,0:T(8,128)S(1)} %fusion.6.position, bf16[16,2,256,256]{3,2,1,0:T(8,128)(2,1)} %block.3, bf16[16,256,256]{2,1,0:T(8,128)(2,1)} %own.1, bf16[16,256,256]{2,1,0:T(8,128)(2,1)} %own.1, ...), custom_call_target="tpu_custom_call" | custom-call | tf_op jit(solution)/shard_map/rotate/pallas_call | solution.py:247
  29.4 0.0 collective-permute-done.5.refs_1_
  29.5 0.7 collective-permute-start.6
  30.1 1.4 %collective-permute-start.7 = (bf16[8,128,128]{2,1,0:T(8,128)(2,1)}, bf16[8,128,128]{2,1,0:T(8,128)(2,1)}, u32[]{:S(2)}, u32[]{:S(2)}) collective-permute-start(bf16[8,128,128]{2,1,0:T(8,128)(2,1)} %collective-permute-done.5.refs_1_), channel_id=1, source_target_pairs={{2,1},{6,5},{10,9},{14,13},{18,17},{22,21},{26,25},{30,29}} | collective-permute-start | bytes 786440 | tf_op jit(solution)/shard_map/ppermute | solution.py:434
  31.5 0.4 collective-permute-done.refs_1_
  31.9 0.7 collective-permute-start.3
  32.6 0.1 copy.14
  32.6 0.7 collective-permute-start.4
  33.3 0.1 fusion.4.target
  33.4 0.0 collective-permute-done.6.refs_2_
  33.4 3.2 %reduce_rows.2 = (f32[4,2,2,2,128,128]{5,4,3,2,1,0:T(8,128)}, bf16[528,128]{1,0:T(8,128)(2,1)S(1)}, bf16[1040,128]{1,0:T(8,128)(2,1)S(1)}, bf16[528,128]{1,0:T(8,128)(2,1)S(1)}, bf16[1040,128]{1,0:T(8,128)(2,1)S(1)}) custom-call(s32[1]{0:T(128)} %bitcast.tcol, s32[16,2]{1,0:T(8,128)S(1)} %fusion.4.target, bf16[8,128,128]{2,1,0:T(8,128)(2,1)} %get-tuple-element.34.refs_0_, ...), custom_call_target="tpu_custom_call" | custom-call | tf_op jit(solution)/shard_map/reduce_rows/pallas_call | solution.py:335
  36.7 7.4 %collective-permute-start.14 = (bf16[528,128]{1,0:T(8,128)(2,1)S(1)}, bf16[528,128]{1,0:T(8,128)(2,1)S(1)}, u32[]{:S(2)}, u32[]{:S(2)}) collective-permute-start(bf16[528,128]{1,0:T(8,128)(2,1)S(1)} %get-tuple-element.47), channel_id=1, source_target_pairs={{0,2},{1,3},{2,0},{3,1},{4,6},{5,7},{6,4},{7,5},{8,10},{9,11},{10,... | collective-permute-start | bytes 405512 | tf_op jit(solution)/shard_map/ppermute | solution.py:31
  44.1 3.6 %collective-permute-start.13 = (bf16[2,256,128]{2,1,0:T(8,128)(2,1)S(1)}, bf16[2,256,128]{2,1,0:T(8,128)(2,1)S(1)}, u32[]{:S(2)}, u32[]{:S(2)}) collective-permute-start(bf16[2,256,128]{2,1,0:T(8,128)(2,1)S(1)} %slice.3), channel_id=1, source_target_pairs={{3,4},{4,3},{7,8},{8,7},{11,12},{12,11},{15,16},{16,15},{19,20},{2... | collective-permute-start | bytes 393224 | tf_op jit(solution)/shard_map/ppermute | solution.py:455
  47.7 0.1 collective-permute-start.11
  47.8 3.8 %collective-permute-start.12 = (bf16[1040,128]{1,0:T(8,128)(2,1)S(1)}, bf16[1040,128]{1,0:T(8,128)(2,1)S(1)}, u32[]{:S(2)}, u32[]{:S(2)}) collective-permute-start(bf16[1040,128]{1,0:T(8,128)(2,1)S(1)} %get-tuple-element.44), channel_id=1, source_target_pairs={{0,3},{1,0},{2,1},{3,2},{4,7},{5,4},{6,5},{7,6},{8,11},{9,8},{10,9... | collective-permute-start | bytes 798728 | tf_op jit(solution)/shard_map/ppermute | solution.py:31
  51.6 2.8 %reduce_rows.3 = (f32[4,2,2,2,128,128]{5,4,3,2,1,0:T(8,128)}, bf16[528,128]{1,0:T(8,128)(2,1)S(1)}, bf16[528,128]{1,0:T(8,128)(2,1)S(1)}, bf16[528,128]{1,0:T(8,128)(2,1)S(1)}, bf16[528,128]{1,0:T(8,128)(2,1)S(1)}) custom-call(s32[1]{0:T(128)} %bitcast.tcol, s32[16,2]{1,0:T(8,128)S(1)} %fusion.4.target, ...), custom_call_target="tpu_custom_call", output_to_operand_aliasing={{0}: (9, {})} | custom-call | tf_op jit(solution)/shard_map/reduce_rows/pallas_call | solution.py:335
  54.4 0.9 %collective-permute-start.10 = (bf16[528,128]{1,0:T(8,128)(2,1)S(1)}, bf16[528,128]{1,0:T(8,128)(2,1)S(1)}, u32[]{:S(2)}, u32[]{:S(2)}) collective-permute-start(bf16[528,128]{1,0:T(8,128)(2,1)S(1)} %get-tuple-element.42), channel_id=1, source_target_pairs={{0,3},{1,0},{2,1},{3,2},{4,7},{5,4},{6,5},{7,6},{8,11},{9,8},{10,9... | collective-permute-start | bytes 405512 | tf_op jit(solution)/shard_map/ppermute | solution.py:31
  55.3 1.1 %collective-permute-start.8 = (bf16[528,128]{1,0:T(8,128)(2,1)S(1)}, bf16[528,128]{1,0:T(8,128)(2,1)S(1)}, u32[]{:S(2)}, u32[]{:S(2)}) collective-permute-start(bf16[528,128]{1,0:T(8,128)(2,1)S(1)} %get-tuple-element.40), channel_id=1, source_target_pairs={{0,1},{1,2},{2,3},{3,0},{4,5},{5,6},{6,7},{7,4},{8,9},{9,10},{10,1... | collective-permute-start | bytes 405512 | tf_op jit(solution)/shard_map/ppermute | solution.py:31
  56.4 4.9 %collective-permute-done.14.refs_2_ = bf16[528,128]{1,0:T(8,128)(2,1)S(1)} collective-permute-done((bf16[528,128]{1,0:T(8,128)(2,1)S(1)}, bf16[528,128]{1,0:T(8,128)(2,1)S(1)}, u32[]{:S(2)}, u32[]{:S(2)}) %collective-permute-start.14) | collective-permute-done | bytes 135200 | tf_op jit(solution)/shard_map/ppermute | solution.py:31
  61.3 3.9 %collective-permute-done.12.refs_3_.refs_5_ = bf16[1040,128]{1,0:T(8,128)(2,1)S(1)} collective-permute-done((bf16[1040,128]{1,0:T(8,128)(2,1)S(1)}, bf16[1040,128]{1,0:T(8,128)(2,1)S(1)}, u32[]{:S(2)}, u32[]{:S(2)}) %collective-permute-start.12) | collective-permute-done | bytes 266272 | tf_op jit(solution)/shard_map/ppermute | solution.py:31
  65.2 7.3 %upper_level.2.refs_8_ = f32[2,5,128,128]{3,2,1,0:T(8,128)} custom-call(s32[1]{0:T(128)} %bitcast.tcol, bf16[528,128]{1,0:T(8,128)(2,1)S(1)} %get-tuple-element.46.refs_0_, bf16[1040,128]{1,0:T(8,128)(2,1)S(1)} %collective-permute-done.11.refs_1_.refs_4_, bf16[528,128]{1,0:T(8,128)(2,1)S(1)} %collective-permute-done.14.refs_2_, ...), custom_call_target="tpu_custom_call" | custom-call | tf_op jit(solution)/shard_map/upper_level/pallas_call | solution.py:398
  72.5 4.8 %collective-permute-done.9.refs_2_ = bf16[528,128]{1,0:T(8,128)(2,1)S(1)} collective-permute-done((bf16[528,128]{1,0:T(8,128)(2,1)S(1)}, bf16[528,128]{1,0:T(8,128)(2,1)S(1)}, u32[]{:S(2)}, u32[]{:S(2)}) %collective-permute-start.9) | collective-permute-done | bytes 135200 | tf_op jit(solution)/shard_map/ppermute | solution.py:31
  77.3 7.2 %upper_level.3 = f32[2,5,128,128]{3,2,1,0:T(8,128)} custom-call(s32[1]{0:T(128)} %bitcast.tcol, bf16[528,128]{1,0:T(8,128)(2,1)S(1)} %get-tuple-element.39.refs_0_, bf16[528,128]{1,0:T(8,128)(2,1)S(1)} %collective-permute-done.8.refs_1_, bf16[528,128]{1,0:T(8,128)(2,1)S(1)} %collective-permute-done.9.refs_2_, ...), custom_call_target="tpu_custom_call", output_to_operand_aliasing={{}: (9, {})} | custom-call | tf_op jit(solution)/shard_map/upper_level/pallas_call | solution.py:398
  (16 shorter events, 0.1 us)
Async XLA Ops:
  1.7 20.0 %collective-permute-start.1 = (bf16[4,256,128]{2,1,0:T(8,128)(2,1)S(1)}, bf16[4,256,128]{2,1,0:T(8,128)(2,1)S(1)}, u32[]{:S(2)}, u32[]{:S(2)}) collective-permute-start(bf16[4,256,128]{2,1,0:T(8,128)(2,1)S(1)} %get-tuple-element.26), channel_id=1, source_target_pairs={{1,5},{2,6},{3,7},{5,9},{6,10},{7,11},{9,13},{10,14},{11,15},{13,1... | collective-permute-start | bytes 786440 | tf_op jit(solution)/shard_map/ppermute | solution.py:36
  2.4 19.4 %collective-permute-start.2 = (bf16[4,256,128]{2,1,0:T(8,128)(2,1)S(1)}, bf16[4,256,128]{2,1,0:T(8,128)(2,1)S(1)}, u32[]{:S(2)}, u32[]{:S(2)}) collective-permute-start(bf16[4,256,128]{2,1,0:T(8,128)(2,1)S(1)} %get-tuple-element.27), channel_id=1, source_target_pairs={{1,29},{2,30},{3,31},{5,1},{6,2},{7,3},{9,5},{10,6},{11,7},{13,9},... | collective-permute-start | bytes 786440 | tf_op jit(solution)/shard_map/ppermute | solution.py:36
  3.1 18.5 %copy-start.1 = (s32[16,2]{0,1:T(2,128)S(1)}, s32[16,2]{0,1:T(2,128)}, u32[]{:S(2)}) copy-start(s32[16,2]{0,1:T(2,128)} %param.7) | copy-start | bytes 388
  18.3 11.1 %collective-permute-start.5 = (bf16[8,128,128]{2,1,0:T(8,128)(2,1)}, bf16[8,128,128]{2,1,0:T(8,128)(2,1)}, u32[]{:S(2)}, u32[]{:S(2)}) collective-permute-start(bf16[8,128,128]{2,1,0:T(8,128)(2,1)} %get-tuple-element.34.refs_0_), channel_id=1, source_target_pairs={{0,2},{4,6},{8,10},{12,14},{16,18},{20,22},{24,26},{28,30}} | collective-permute-start | bytes 786440 | tf_op jit(solution)/shard_map/ppermute | solution.py:434
  20.3 11.6 %collective-permute-start = (bf16[8,128,128]{2,1,0:T(8,128)(2,1)S(1)}, bf16[8,128,128]{2,1,0:T(8,128)(2,1)S(1)}, u32[]{:S(2)}, u32[]{:S(2)}) collective-permute-start(bf16[8,128,128]{2,1,0:T(8,128)(2,1)S(1)} %get-tuple-element.25.refs_0_), channel_id=1, source_target_pairs={{0,2},{4,6},{8,10},{12,14},{16,18},{20,22},{24,26},{28,30}} | collective-permute-start | bytes 786440 | tf_op jit(solution)/shard_map/ppermute | solution.py:434
  21.7 11.7 %copy-start = (bf16[2,256,256]{2,1,0:T(8,128)(2,1)S(1)}, bf16[2,256,256]{2,1,0:T(8,128)(2,1)}, u32[]{:S(2)}) copy-start(bf16[2,256,256]{2,1,0:T(8,128)(2,1)} %refs_7_.5) | copy-start | bytes 786436
  29.5 4.0 %collective-permute-start.6 = (bf16[8,128,128]{2,1,0:T(8,128)(2,1)}, bf16[8,128,128]{2,1,0:T(8,128)(2,1)S(1)}, u32[]{:S(2)}, u32[]{:S(2)}) collective-permute-start(bf16[8,128,128]{2,1,0:T(8,128)(2,1)} %collective-permute-done.5.refs_1_), channel_id=1, source_target_pairs={{2,3},{6,7},{10,11},{14,15},{18,19},{22,23},{26,27},{30,31}} | collective-permute-start | bytes 786440 | tf_op jit(solution)/shard_map/ppermute | solution.py:434
  30.1 3.3 %collective-permute-start.7 = (bf16[8,128,128]{2,1,0:T(8,128)(2,1)}, bf16[8,128,128]{2,1,0:T(8,128)(2,1)}, u32[]{:S(2)}, u32[]{:S(2)}) collective-permute-start(bf16[8,128,128]{2,1,0:T(8,128)(2,1)} %collective-permute-done.5.refs_1_), channel_id=1, source_target_pairs={{2,1},{6,5},{10,9},{14,13},{18,17},{22,21},{26,25},{30,29}} | collective-permute-start | bytes 786440 | tf_op jit(solution)/shard_map/ppermute | solution.py:434
  31.9 15.9 %collective-permute-start.3 = (bf16[8,128,128]{2,1,0:T(8,128)(2,1)S(1)}, bf16[8,128,128]{2,1,0:T(8,128)(2,1)S(1)}, u32[]{:S(2)}, u32[]{:S(2)}) collective-permute-start(bf16[8,128,128]{2,1,0:T(8,128)(2,1)S(1)} %collective-permute-done.refs_1_), channel_id=1, source_target_pairs={{2,3},{6,7},{10,11},{14,15},{18,19},{22,23},{26,27},{30,31}} | collective-permute-start | bytes 786440 | tf_op jit(solution)/shard_map/ppermute | solution.py:434
  32.6 19.0 %collective-permute-start.4 = (bf16[8,128,128]{2,1,0:T(8,128)(2,1)S(1)}, bf16[8,128,128]{2,1,0:T(8,128)(2,1)S(1)}, u32[]{:S(2)}, u32[]{:S(2)}) collective-permute-start(bf16[8,128,128]{2,1,0:T(8,128)(2,1)S(1)} %collective-permute-done.refs_1_), channel_id=1, source_target_pairs={{2,1},{6,5},{10,9},{14,13},{18,17},{22,21},{26,25},{30,29}} | collective-permute-start | bytes 786440 | tf_op jit(solution)/shard_map/ppermute | solution.py:434
  36.7 24.6 %collective-permute-start.14 = (bf16[528,128]{1,0:T(8,128)(2,1)S(1)}, bf16[528,128]{1,0:T(8,128)(2,1)S(1)}, u32[]{:S(2)}, u32[]{:S(2)}) collective-permute-start(bf16[528,128]{1,0:T(8,128)(2,1)S(1)} %get-tuple-element.47), channel_id=1, source_target_pairs={{0,2},{1,3},{2,0},{3,1},{4,6},{5,7},{6,4},{7,5},{8,10},{9,11},{10,... | collective-permute-start | bytes 405512 | tf_op jit(solution)/shard_map/ppermute | solution.py:31
  44.1 11.2 %collective-permute-start.13 = (bf16[2,256,128]{2,1,0:T(8,128)(2,1)S(1)}, bf16[2,256,128]{2,1,0:T(8,128)(2,1)S(1)}, u32[]{:S(2)}, u32[]{:S(2)}) collective-permute-start(bf16[2,256,128]{2,1,0:T(8,128)(2,1)S(1)} %slice.3), channel_id=1, source_target_pairs={{3,4},{4,3},{7,8},{8,7},{11,12},{12,11},{15,16},{16,15},{19,20},{2... | collective-permute-start | bytes 393224 | tf_op jit(solution)/shard_map/ppermute | solution.py:455
  47.7 13.6 %collective-permute-start.11 = (bf16[1040,128]{1,0:T(8,128)(2,1)S(1)}, bf16[1040,128]{1,0:T(8,128)(2,1)S(1)}, u32[]{:S(2)}, u32[]{:S(2)}) collective-permute-start(bf16[1040,128]{1,0:T(8,128)(2,1)S(1)} %get-tuple-element.43), channel_id=1, source_target_pairs={{0,1},{1,2},{2,3},{3,0},{4,5},{5,6},{6,7},{7,4},{8,9},{9,10},{10,1... | collective-permute-start | bytes 798728 | tf_op jit(solution)/shard_map/ppermute | solution.py:31
  47.8 17.4 %collective-permute-start.12 = (bf16[1040,128]{1,0:T(8,128)(2,1)S(1)}, bf16[1040,128]{1,0:T(8,128)(2,1)S(1)}, u32[]{:S(2)}, u32[]{:S(2)}) collective-permute-start(bf16[1040,128]{1,0:T(8,128)(2,1)S(1)} %get-tuple-element.44), channel_id=1, source_target_pairs={{0,3},{1,0},{2,1},{3,2},{4,7},{5,4},{6,5},{7,6},{8,11},{9,8},{10,9... | collective-permute-start | bytes 798728 | tf_op jit(solution)/shard_map/ppermute | solution.py:31
  54.4 18.1 %collective-permute-start.10 = (bf16[528,128]{1,0:T(8,128)(2,1)S(1)}, bf16[528,128]{1,0:T(8,128)(2,1)S(1)}, u32[]{:S(2)}, u32[]{:S(2)}) collective-permute-start(bf16[528,128]{1,0:T(8,128)(2,1)S(1)} %get-tuple-element.42), channel_id=1, source_target_pairs={{0,3},{1,0},{2,1},{3,2},{4,7},{5,4},{6,5},{7,6},{8,11},{9,8},{10,9... | collective-permute-start | bytes 405512 | tf_op jit(solution)/shard_map/ppermute | solution.py:31
  55.3 17.2 %collective-permute-start.8 = (bf16[528,128]{1,0:T(8,128)(2,1)S(1)}, bf16[528,128]{1,0:T(8,128)(2,1)S(1)}, u32[]{:S(2)}, u32[]{:S(2)}) collective-permute-start(bf16[528,128]{1,0:T(8,128)(2,1)S(1)} %get-tuple-element.40), channel_id=1, source_target_pairs={{0,1},{1,2},{2,3},{3,0},{4,5},{5,6},{6,7},{7,4},{8,9},{9,10},{10,1... | collective-permute-start | bytes 405512 | tf_op jit(solution)/shard_map/ppermute | solution.py:31
  61.3 16.0 %collective-permute-start.9 = (bf16[528,128]{1,0:T(8,128)(2,1)S(1)}, bf16[528,128]{1,0:T(8,128)(2,1)S(1)}, u32[]{:S(2)}, u32[]{:S(2)}) collective-permute-start(bf16[528,128]{1,0:T(8,128)(2,1)S(1)} %get-tuple-element.41), channel_id=1, source_target_pairs={{0,2},{1,3},{2,0},{3,1},{4,6},{5,7},{6,4},{7,5},{8,10},{9,11},{10,... | collective-permute-start | bytes 405512 | tf_op jit(solution)/shard_map/ppermute | solution.py:31

commit v3 on v2

--- a/solution.py
+++ b/solution.py
@@ -157,6 +157,40 @@
         compiler_params=PARAMS,
         name="ends",
     )(bases)
+
+
+def solve_one(left, right, size, order):
+    ids = lax.broadcasted_iota(jnp.int32, (order, 1), 0)
+    for lo in range(0, size, order):
+        hi = lo + order
+        last = hi == size
+        x = [left[lo:hi, :], right[lo:hi, :]]
+        for s in range(0, order, SUB):
+            cols = [
+                jnp.broadcast_to(x[0][:, lo + s + c : lo + s + c + 1], (order, LANES))
+                for c in range(SUB)
+            ]
+            for c in range(SUB):
+                p = s + c
+                pivot = 1.0 / cols[c][p : p + 1, :]
+                here = ids == p
+                col = jnp.where(here, 0.0, cols[c])
+                for e in range(c + 1, SUB):
+                    row = cols[e][p : p + 1, :] * pivot
+                    cols[e] = jnp.where(here, row, cols[e] - col * row)
+                for h in range(2):
+                    row = x[h][p : p + 1, :] * pivot
+                    x[h] = jnp.where(here, row, x[h] - col * row)
+        panel = x[1] if last else jnp.concatenate(x, axis=1)
+        for start, stop in ((0, lo), (hi, size)):
+            if start < stop:
+                update = dot3(left[start:stop, lo:hi], panel)
+                if not last:
+                    left[start:stop, :] -= update[:, :size]
+                right[start:stop, :] -= update[:, -size:]
+        if not last:
+            left[lo:hi, :] = x[0]
+        right[lo:hi, :] = x[1]
 
 
 def factor_kernel(count, group, owned, tcol, block, basis, *refs):
@@ -352,7 +386,7 @@
 
 def upper_kernel(parent, parents, tcols, slots, tcol, *refs):
     arrivals, (before, later, edge, basis) = refs[:tcols], refs[tcols : tcols + 4]
-    out, merged, left, right, inverse = refs[-5:]
+    out, merged, left, right = refs[-4:]
     merged[...] = jnp.zeros_like(merged)
     end = 2 * slots * RANK + TAIL
     for arrival in arrivals:
@@ -378,9 +412,9 @@
         mixed.append(dot(pair, other).astype(BF16))
     lifted = dot_t(basis[parent], jnp.concatenate(mixed, axis=1))
     corner = lifted[:RANK, :RANK]
-    left[:RANK, :] = 0.5 * (corner + jnp.transpose(corner))
+    left[...] = 0.5 * (corner + jnp.transpose(corner))
     right[...] = lifted[:RANK, RANK : 2 * RANK]
-    solve_spd(left, right, inverse, 1, RANK, UPPER_PANEL)
+    solve_one(left, right, RANK, UPPER_PANEL)
     result = lifted[RANK:, RANK:] - dot3(jnp.transpose(right[...]), lifted[:RANK, RANK:])
     for place, d in enumerate((2, 0, 1, 3, 4)):
         out[0, d] = result[:, place * RANK : (place + 1) * RANK]
@@ -402,7 +436,7 @@
         out_specs=pl.BlockSpec((1, 5, RANK, RANK), lambda i: (parent, 0, 0, 0)),
         out_shape=jax.ShapeDtypeStruct((parents, 5, RANK, RANK), F32),
         input_output_aliases=aliases,
-        scratch_shapes=[VMEM((10, 2 * RANK, RANK), BF16)] + solve_scratch(1, RANK, UPPER_PANEL),
+        scratch_shapes=[VMEM((10, 2 * RANK, RANK), BF16)] + [VMEM((RANK, RANK), F32)] * 2,
         compiler_params=PARAMS,
         name="upper_level",
     )(*operands)
@@ -453,6 +487,7 @@
         first %= lax.axis_size(everyone)
         pairs += [(last, first), (first, last)]
     edge = lax.ppermute(after(upper_bases, *parts)[:, :, RANK:], everyone, pairs)
+    target = after(target, edge)
 
     skeleton = None
     arrivals = []

time: 85.6 us -> 82 us (0.958)
  waiting for transfers between devices: 14 us -> 23 us
  starting transfers between devices: 25 us -> 17 us
  Pallas kernels: 44.5 us -> 40.4 us
    ppermute x6, starting transfers between devices: 13.3 us -> 5.75 us  [ring(): lax.ppermute(array, axes, [(i, (i + step) % count) for i in range(count)])]
    ppermute x1, waiting for transfers between devices: 0.01 us -> 7.3 us  [per_device(): lax.ppermute(after(upper_bases, *parts)[:, :, RANK:], everyone, pairs)]
    pallas_call x2, Pallas kernels: 14.5 us -> 10.5 us  [upper_level(): pl.pallas_call(functools.partial(upper_kernel, parent, parents, len(arriv...]
    ppermute x6, waiting for transfers between devices: 13.6 us -> 14.7 us  [ring(): lax.ppermute(array, axes, [(i, (i + step) % count) for i in range(count)])]
  transfers between devices with their start and end apart: 15 -> 15, of which waited for: 4 -> 5; matrix products, arithmetic and copies ran while one was open for 0% -> 0% of each run, Pallas kernels for 43% -> 42%
where the time goes in v3:
time: 82 us; the launch traced here: 81.5 us
  Pallas kernels  40.4 us (49%)
  waiting for transfers between devices  23 us (28%)
  starting transfers between devices  17 us (21%)
    pallas_call x1, Pallas kernels, factor(): pl.pallas_call(functools.partial(factor_kernel, count, group, owned), gri...  15.2 us
    ppermute x6, waiting for transfers between devices, ring(): lax.ppermute(array, axes, [(i, (i + step) % count) for i in range(count)])  14.7 us
    pallas_call x2, Pallas kernels, upper_level(): pl.pallas_call(functools.partial(upper_kernel, parent, parents, len(arriv...  10.5 us
    pallas_call x1, Pallas kernels, rotate(): pl.pallas_call(functools.partial(rotate_kernel, slots, owned), grid=(coun...  7.68 us
    ppermute x1, waiting for transfers between devices, per_device(): lax.ppermute(after(upper_bases, *parts)[:, :, RANK:], everyone, pairs)  7.3 us
    ppermute x6, starting transfers between devices, per_device(): lax.ppermute(array, 'tcol', [(start, stop)])  5.98 us
    pallas_call x2, Pallas kernels, reduce_rows(): pl.pallas_call(functools.partial(reduce_kernel, part, slots, half, places...  5.9 us
    ppermute x6, starting transfers between devices, ring(): lax.ppermute(array, axes, [(i, (i + step) % count) for i in range(count)])  5.75 us
  transfers between devices with their start and end apart: 15, of which 5 were waited for; matrix products, arithmetic and copies ran while one was open for 0% of the time, Pallas kernels for 42%

profile of v3, /device:TPU:0, one launch (start us, length us, event | category | flops | bytes accessed | tf_op | source)
XLA Modules:
  0.0 81.5 jit_solution(12219342489608306484)
XLA Ops:
  0.6 1.1 %ends.1 = (bf16[4,256,128]{2,1,0:T(8,128)(2,1)S(1)}, bf16[4,256,128]{2,1,0:T(8,128)(2,1)S(1)}) custom-call(bf16[16,256,256]{2,1,0:T(8,128)(2,1)} %basis.5), custom_call_target="tpu_custom_call" | custom-call | tf_op jit(solution)/shard_map/ends/pallas_call | solution.py:151
  1.7 0.7 collective-permute-start
  2.4 0.7 collective-permute-start.1
  3.1 0.0 copy-start.1
  3.1 15.2 %factor.1 = (bf16[8,128,128]{2,1,0:T(8,128)(2,1)}, bf16[8,128,128]{2,1,0:T(8,128)(2,1)}, bf16[8,128,128]{2,1,0:T(8,128)(2,1)S(1)}, bf16[8,128,128]{2,1,0:T(8,128)(2,1)}) custom-call(s32[1]{0:T(128)} %bitcast.tcol, bf16[16,2,256,256]{3,2,1,0:T(8,128)(2,1)} %block.3, bf16[16,256,256]{2,1,0:T(8,128)(2,1)} %basis.5), custom_call_target="tpu_custom_call" | custom-call | tf_op jit(solution)/shard_map/factor/pallas_call | solution.py:227
  18.3 2.0 %collective-permute-start.6 = (bf16[8,128,128]{2,1,0:T(8,128)(2,1)}, bf16[8,128,128]{2,1,0:T(8,128)(2,1)}, u32[]{:S(2)}, u32[]{:S(2)}) collective-permute-start(bf16[8,128,128]{2,1,0:T(8,128)(2,1)} %get-tuple-element.37.refs_0_), channel_id=1, source_target_pairs={{0,2},{4,6},{8,10},{12,14},{16,18},{20,22},{24,26},{28,30}} | collective-permute-start | bytes 786440 | tf_op jit(solution)/shard_map/ppermute | solution.py:468
  20.3 1.3 %collective-permute-start.3 = (bf16[8,128,128]{2,1,0:T(8,128)(2,1)S(1)}, bf16[8,128,128]{2,1,0:T(8,128)(2,1)S(1)}, u32[]{:S(2)}, u32[]{:S(2)}) collective-permute-start(bf16[8,128,128]{2,1,0:T(8,128)(2,1)S(1)} %get-tuple-element.34.refs_0_), channel_id=1, source_target_pairs={{0,2},{4,6},{8,10},{12,14},{16,18},{20,22},{24,26},{28,30}} | collective-permute-start | bytes 786440 | tf_op jit(solution)/shard_map/ppermute | solution.py:468
  21.6 0.1 copy.18
  21.7 0.0 collective-permute-done.before
  21.8 7.7 %rotate.1 = (bf16[8,256,256]{2,1,0:T(8,128)(2,1)S(1)}, f32[8,128,256]{2,1,0:T(8,128)}, bf16[8,256,256]{2,1,0:T(8,128)(2,1)S(1)}, f32[8,128,256]{2,1,0:T(8,128)}) custom-call(s32[16,2]{1,0:T(8,128)S(1)} %fusion.6.position, bf16[16,2,256,256]{3,2,1,0:T(8,128)(2,1)} %block.3, bf16[16,256,256]{2,1,0:T(8,128)(2,1)} %basis.5, bf16[16,256,256]{2,1,0:T(8,128)(2,1)} %basis.5, ...), custom_call_target="tpu_custom_call" | custom-call | tf_op jit(solution)/shard_map/rotate/pallas_call | solution.py:281
  29.5 0.7 collective-permute-start.7
  30.1 0.7 collective-permute-start.8
  30.8 0.1 copy.14
  30.9 0.9 %collective-permute-done.3.refs_1_ = bf16[8,128,128]{2,1,0:T(8,128)(2,1)S(1)} collective-permute-done((bf16[8,128,128]{2,1,0:T(8,128)(2,1)S(1)}, bf16[8,128,128]{2,1,0:T(8,128)(2,1)S(1)}, u32[]{:S(2)}, u32[]{:S(2)}) %collective-permute-start.3) | collective-permute-done | bytes 262176 | tf_op jit(solution)/shard_map/ppermute | solution.py:468
  31.9 0.7 collective-permute-start.4
  32.5 0.7 collective-permute-start.5
  33.3 3.9 %collective-permute-start.2 = (bf16[2,256,128]{2,1,0:T(8,128)(2,1)S(1)}, bf16[2,256,128]{2,1,0:T(8,128)(2,1)S(1)}, u32[]{:S(2)}, u32[]{:S(2)}) collective-permute-start(bf16[2,256,128]{2,1,0:T(8,128)(2,1)S(1)} %slice.3), channel_id=1, source_target_pairs={{3,4},{4,3},{7,8},{8,7},{11,12},{12,11},{15,16},{16,15},{19,20},{2... | collective-permute-start | bytes 393224 | tf_op jit(solution)/shard_map/ppermute | solution.py:489
  37.2 0.1 fusion.4.target
  37.3 7.3 %collective-permute-done.2.refs_6_ = bf16[2,256,128]{2,1,0:T(8,128)(2,1)S(1)} collective-permute-done((bf16[2,256,128]{2,1,0:T(8,128)(2,1)S(1)}, bf16[2,256,128]{2,1,0:T(8,128)(2,1)S(1)}, u32[]{:S(2)}, u32[]{:S(2)}) %collective-permute-start.2) | collective-permute-done | bytes 131104 | tf_op jit(solution)/shard_map/ppermute | solution.py:489
  44.6 0.0 collective-permute-done.7.refs_2_
  44.6 0.0 collective-permute-done.8.refs_3_
  44.6 3.1 %reduce_rows.2 = (f32[4,2,2,2,128,128]{5,4,3,2,1,0:T(8,128)}, bf16[528,128]{1,0:T(8,128)(2,1)S(1)}, bf16[1040,128]{1,0:T(8,128)(2,1)S(1)}, bf16[528,128]{1,0:T(8,128)(2,1)S(1)}, bf16[1040,128]{1,0:T(8,128)(2,1)S(1)}) custom-call(s32[1]{0:T(128)} %bitcast.tcol, s32[16,2]{1,0:T(8,128)S(1)} %fusion.4.target, bf16[8,128,128]{2,1,0:T(8,128)(2,1)} %get-tuple-element.37.refs_0_, ...), custom_call_target="tpu_custom_call" | custom-call | tf_op jit(solution)/shard_map/reduce_rows/pallas_call | solution.py:369
  47.7 0.5 collective-permute-start.12
  48.3 3.3 %collective-permute-start.13 = (bf16[1040,128]{1,0:T(8,128)(2,1)S(1)}, bf16[1040,128]{1,0:T(8,128)(2,1)S(1)}, u32[]{:S(2)}, u32[]{:S(2)}) collective-permute-start(bf16[1040,128]{1,0:T(8,128)(2,1)S(1)} %get-tuple-element.47), channel_id=1, source_target_pairs={{0,3},{1,0},{2,1},{3,2},{4,7},{5,4},{6,5},{7,6},{8,11},{9,8},{10,9... | collective-permute-start | bytes 798728 | tf_op jit(solution)/shard_map/ppermute | solution.py:31
  51.6 2.8 %reduce_rows.3 = (f32[4,2,2,2,128,128]{5,4,3,2,1,0:T(8,128)}, bf16[528,128]{1,0:T(8,128)(2,1)S(1)}, bf16[528,128]{1,0:T(8,128)(2,1)S(1)}, bf16[528,128]{1,0:T(8,128)(2,1)S(1)}, bf16[528,128]{1,0:T(8,128)(2,1)S(1)}) custom-call(s32[1]{0:T(128)} %bitcast.tcol, s32[16,2]{1,0:T(8,128)S(1)} %fusion.4.target, ...), custom_call_target="tpu_custom_call", output_to_operand_aliasing={{0}: (9, {})} | custom-call | tf_op jit(solution)/shard_map/reduce_rows/pallas_call | solution.py:369
  54.3 1.0 %collective-permute-start.10 = (bf16[528,128]{1,0:T(8,128)(2,1)S(1)}, bf16[528,128]{1,0:T(8,128)(2,1)S(1)}, u32[]{:S(2)}, u32[]{:S(2)}) collective-permute-start(bf16[528,128]{1,0:T(8,128)(2,1)S(1)} %get-tuple-element.44), channel_id=1, source_target_pairs={{0,2},{1,3},{2,0},{3,1},{4,6},{5,7},{6,4},{7,5},{8,10},{9,11},{10,... | collective-permute-start | bytes 405512 | tf_op jit(solution)/shard_map/ppermute | solution.py:31
  55.3 0.9 %collective-permute-start.11 = (bf16[528,128]{1,0:T(8,128)(2,1)S(1)}, bf16[528,128]{1,0:T(8,128)(2,1)S(1)}, u32[]{:S(2)}, u32[]{:S(2)}) collective-permute-start(bf16[528,128]{1,0:T(8,128)(2,1)S(1)} %get-tuple-element.45), channel_id=1, source_target_pairs={{0,3},{1,0},{2,1},{3,2},{4,7},{5,4},{6,5},{7,6},{8,11},{9,8},{10,9... | collective-permute-start | bytes 405512 | tf_op jit(solution)/shard_map/ppermute | solution.py:31
  56.3 5.6 %collective-permute-done.14.refs_2_ = bf16[528,128]{1,0:T(8,128)(2,1)S(1)} collective-permute-done((bf16[528,128]{1,0:T(8,128)(2,1)S(1)}, bf16[528,128]{1,0:T(8,128)(2,1)S(1)}, u32[]{:S(2)}, u32[]{:S(2)}) %collective-permute-start.14) | collective-permute-done | bytes 135200 | tf_op jit(solution)/shard_map/ppermute | solution.py:31
  61.9 4.4 %collective-permute-done.13.refs_3_.refs_5_ = bf16[1040,128]{1,0:T(8,128)(2,1)S(1)} collective-permute-done((bf16[1040,128]{1,0:T(8,128)(2,1)S(1)}, bf16[1040,128]{1,0:T(8,128)(2,1)S(1)}, u32[]{:S(2)}, u32[]{:S(2)}) %collective-permute-start.13) | collective-permute-done | bytes 266272 | tf_op jit(solution)/shard_map/ppermute | solution.py:31
  66.3 5.3 %upper_level.2.refs_8_ = f32[2,5,128,128]{3,2,1,0:T(8,128)} custom-call(s32[1]{0:T(128)} %bitcast.tcol, bf16[528,128]{1,0:T(8,128)(2,1)S(1)} %get-tuple-element.48.refs_0_, bf16[1040,128]{1,0:T(8,128)(2,1)S(1)} %collective-permute-done.12.refs_1_.refs_4_, bf16[528,128]{1,0:T(8,128)(2,1)S(1)} %collective-permute-done.14.refs_2_, ...), custom_call_target="tpu_custom_call" | custom-call | tf_op jit(solution)/shard_map/upper_level/pallas_call | solution.py:432
  71.5 4.7 %collective-permute-done.10.refs_2_ = bf16[528,128]{1,0:T(8,128)(2,1)S(1)} collective-permute-done((bf16[528,128]{1,0:T(8,128)(2,1)S(1)}, bf16[528,128]{1,0:T(8,128)(2,1)S(1)}, u32[]{:S(2)}, u32[]{:S(2)}) %collective-permute-start.10) | collective-permute-done | bytes 135200 | tf_op jit(solution)/shard_map/ppermute | solution.py:31
  76.3 5.3 %upper_level.3 = f32[2,5,128,128]{3,2,1,0:T(8,128)} custom-call(s32[1]{0:T(128)} %bitcast.tcol, bf16[528,128]{1,0:T(8,128)(2,1)S(1)} %get-tuple-element.42.refs_0_, bf16[528,128]{1,0:T(8,128)(2,1)S(1)} %collective-permute-done.9.refs_1_, bf16[528,128]{1,0:T(8,128)(2,1)S(1)} %collective-permute-done.10.refs_2_, ...), custom_call_target="tpu_custom_call", output_to_operand_aliasing={{}: (9, {})} | custom-call | tf_op jit(solution)/shard_map/upper_level/pallas_call | solution.py:432
  (16 shorter events, 0.1 us)
Async XLA Ops:
  1.7 20.0 %collective-permute-start = (bf16[4,256,128]{2,1,0:T(8,128)(2,1)S(1)}, bf16[4,256,128]{2,1,0:T(8,128)(2,1)S(1)}, u32[]{:S(2)}, u32[]{:S(2)}) collective-permute-start(bf16[4,256,128]{2,1,0:T(8,128)(2,1)S(1)} %get-tuple-element.26), channel_id=1, source_target_pairs={{1,5},{2,6},{3,7},{5,9},{6,10},{7,11},{9,13},{10,14},{11,15},{13,1... | collective-permute-start | bytes 786440 | tf_op jit(solution)/shard_map/ppermute | solution.py:36
  2.4 19.4 %collective-permute-start.1 = (bf16[4,256,128]{2,1,0:T(8,128)(2,1)S(1)}, bf16[4,256,128]{2,1,0:T(8,128)(2,1)S(1)}, u32[]{:S(2)}, u32[]{:S(2)}) collective-permute-start(bf16[4,256,128]{2,1,0:T(8,128)(2,1)S(1)} %get-tuple-element.27), channel_id=1, source_target_pairs={{1,29},{2,30},{3,31},{5,1},{6,2},{7,3},{9,5},{10,6},{11,7},{13,9},... | collective-permute-start | bytes 786440 | tf_op jit(solution)/shard_map/ppermute | solution.py:36
  3.1 18.5 %copy-start.1 = (s32[16,2]{0,1:T(2,128)S(1)}, s32[16,2]{0,1:T(2,128)}, u32[]{:S(2)}) copy-start(s32[16,2]{0,1:T(2,128)} %param.7) | copy-start | bytes 388
  18.3 11.1 %collective-permute-start.6 = (bf16[8,128,128]{2,1,0:T(8,128)(2,1)}, bf16[8,128,128]{2,1,0:T(8,128)(2,1)}, u32[]{:S(2)}, u32[]{:S(2)}) collective-permute-start(bf16[8,128,128]{2,1,0:T(8,128)(2,1)} %get-tuple-element.37.refs_0_), channel_id=1, source_target_pairs={{0,2},{4,6},{8,10},{12,14},{16,18},{20,22},{24,26},{28,30}} | collective-permute-start | bytes 786440 | tf_op jit(solution)/shard_map/ppermute | solution.py:468
  20.3 11.6 %collective-permute-start.3 = (bf16[8,128,128]{2,1,0:T(8,128)(2,1)S(1)}, bf16[8,128,128]{2,1,0:T(8,128)(2,1)S(1)}, u32[]{:S(2)}, u32[]{:S(2)}) collective-permute-start(bf16[8,128,128]{2,1,0:T(8,128)(2,1)S(1)} %get-tuple-element.34.refs_0_), channel_id=1, source_target_pairs={{0,2},{4,6},{8,10},{12,14},{16,18},{20,22},{24,26},{28,30}} | collective-permute-start | bytes 786440 | tf_op jit(solution)/shard_map/ppermute | solution.py:468
  21.7 11.5 %copy-start = (bf16[2,256,256]{2,1,0:T(8,128)(2,1)S(1)}, bf16[2,256,256]{2,1,0:T(8,128)(2,1)}, u32[]{:S(2)}) copy-start(bf16[2,256,256]{2,1,0:T(8,128)(2,1)} %refs_7_.5) | copy-start | bytes 786436
  29.5 15.1 %collective-permute-start.7 = (bf16[8,128,128]{2,1,0:T(8,128)(2,1)}, bf16[8,128,128]{2,1,0:T(8,128)(2,1)S(1)}, u32[]{:S(2)}, u32[]{:S(2)}) collective-permute-start(bf16[8,128,128]{2,1,0:T(8,128)(2,1)} %collective-permute-done.6.refs_1_), channel_id=1, source_target_pairs={{2,3},{6,7},{10,11},{14,15},{18,19},{22,23},{26,27},{30,31}} | collective-permute-start | bytes 786440 | tf_op jit(solution)/shard_map/ppermute | solution.py:468
  30.1 14.5 %collective-permute-start.8 = (bf16[8,128,128]{2,1,0:T(8,128)(2,1)}, bf16[8,128,128]{2,1,0:T(8,128)(2,1)S(1)}, u32[]{:S(2)}, u32[]{:S(2)}) collective-permute-start(bf16[8,128,128]{2,1,0:T(8,128)(2,1)} %collective-permute-done.6.refs_1_), channel_id=1, source_target_pairs={{2,1},{6,5},{10,9},{14,13},{18,17},{22,21},{26,25},{30,29}} | collective-permute-start | bytes 786440 | tf_op jit(solution)/shard_map/ppermute | solution.py:468
  31.9 19.7 %collective-permute-start.4 = (bf16[8,128,128]{2,1,0:T(8,128)(2,1)S(1)}, bf16[8,128,128]{2,1,0:T(8,128)(2,1)S(1)}, u32[]{:S(2)}, u32[]{:S(2)}) collective-permute-start(bf16[8,128,128]{2,1,0:T(8,128)(2,1)S(1)} %collective-permute-done.3.refs_1_), channel_id=1, source_target_pairs={{2,3},{6,7},{10,11},{14,15},{18,19},{22,23},{26,27},{30,31}} | collective-permute-start | bytes 786440 | tf_op jit(solution)/shard_map/ppermute | solution.py:468
  32.5 19.0 %collective-permute-start.5 = (bf16[8,128,128]{2,1,0:T(8,128)(2,1)S(1)}, bf16[8,128,128]{2,1,0:T(8,128)(2,1)S(1)}, u32[]{:S(2)}, u32[]{:S(2)}) collective-permute-start(bf16[8,128,128]{2,1,0:T(8,128)(2,1)S(1)} %collective-permute-done.3.refs_1_), channel_id=1, source_target_pairs={{2,1},{6,5},{10,9},{14,13},{18,17},{22,21},{26,25},{30,29}} | collective-permute-start | bytes 786440 | tf_op jit(solution)/shard_map/ppermute | solution.py:468
  33.3 11.3 %collective-permute-start.2 = (bf16[2,256,128]{2,1,0:T(8,128)(2,1)S(1)}, bf16[2,256,128]{2,1,0:T(8,128)(2,1)S(1)}, u32[]{:S(2)}, u32[]{:S(2)}) collective-permute-start(bf16[2,256,128]{2,1,0:T(8,128)(2,1)S(1)} %slice.3), channel_id=1, source_target_pairs={{3,4},{4,3},{7,8},{8,7},{11,12},{12,11},{15,16},{16,15},{19,20},{2... | collective-permute-start | bytes 393224 | tf_op jit(solution)/shard_map/ppermute | solution.py:489
  47.7 14.1 %collective-permute-start.14 = (bf16[528,128]{1,0:T(8,128)(2,1)S(1)}, bf16[528,128]{1,0:T(8,128)(2,1)S(1)}, u32[]{:S(2)}, u32[]{:S(2)}) collective-permute-start(bf16[528,128]{1,0:T(8,128)(2,1)S(1)} %get-tuple-element.49), channel_id=1, source_target_pairs={{0,2},{1,3},{2,0},{3,1},{4,6},{5,7},{6,4},{7,5},{8,10},{9,11},{10,... | collective-permute-start | bytes 405512 | tf_op jit(solution)/shard_map/ppermute | solution.py:31
  47.7 14.1 %collective-permute-start.12 = (bf16[1040,128]{1,0:T(8,128)(2,1)S(1)}, bf16[1040,128]{1,0:T(8,128)(2,1)S(1)}, u32[]{:S(2)}, u32[]{:S(2)}) collective-permute-start(bf16[1040,128]{1,0:T(8,128)(2,1)S(1)} %get-tuple-element.46), channel_id=1, source_target_pairs={{0,1},{1,2},{2,3},{3,0},{4,5},{5,6},{6,7},{7,4},{8,9},{9,10},{10,1... | collective-permute-start | bytes 798728 | tf_op jit(solution)/shard_map/ppermute | solution.py:31
  48.3 18.0 %collective-permute-start.13 = (bf16[1040,128]{1,0:T(8,128)(2,1)S(1)}, bf16[1040,128]{1,0:T(8,128)(2,1)S(1)}, u32[]{:S(2)}, u32[]{:S(2)}) collective-permute-start(bf16[1040,128]{1,0:T(8,128)(2,1)S(1)} %get-tuple-element.47), channel_id=1, source_target_pairs={{0,3},{1,0},{2,1},{3,2},{4,7},{5,4},{6,5},{7,6},{8,11},{9,8},{10,9... | collective-permute-start | bytes 798728 | tf_op jit(solution)/shard_map/ppermute | solution.py:31
  54.3 21.9 %collective-permute-start.10 = (bf16[528,128]{1,0:T(8,128)(2,1)S(1)}, bf16[528,128]{1,0:T(8,128)(2,1)S(1)}, u32[]{:S(2)}, u32[]{:S(2)}) collective-permute-start(bf16[528,128]{1,0:T(8,128)(2,1)S(1)} %get-tuple-element.44), channel_id=1, source_target_pairs={{0,2},{1,3},{2,0},{3,1},{4,6},{5,7},{6,4},{7,5},{8,10},{9,11},{10,... | collective-permute-start | bytes 405512 | tf_op jit(solution)/shard_map/ppermute | solution.py:31
  55.3 20.9 %collective-permute-start.11 = (bf16[528,128]{1,0:T(8,128)(2,1)S(1)}, bf16[528,128]{1,0:T(8,128)(2,1)S(1)}, u32[]{:S(2)}, u32[]{:S(2)}) collective-permute-start(bf16[528,128]{1,0:T(8,128)(2,1)S(1)} %get-tuple-element.45), channel_id=1, source_target_pairs={{0,3},{1,0},{2,1},{3,2},{4,7},{5,4},{6,5},{7,6},{8,11},{9,8},{10,9... | collective-permute-start | bytes 405512 | tf_op jit(solution)/shard_map/ppermute | solution.py:31
  61.9 14.4 %collective-permute-start.9 = (bf16[528,128]{1,0:T(8,128)(2,1)S(1)}, bf16[528,128]{1,0:T(8,128)(2,1)S(1)}, u32[]{:S(2)}, u32[]{:S(2)}) collective-permute-start(bf16[528,128]{1,0:T(8,128)(2,1)S(1)} %get-tuple-element.43), channel_id=1, source_target_pairs={{0,1},{1,2},{2,3},{3,0},{4,5},{5,6},{6,7},{7,4},{8,9},{9,10},{10,1... | collective-permute-start | bytes 405512 | tf_op jit(solution)/shard_map/ppermute | solution.py:31
